TPU v7x, 512 devices: a whole 4x4x16 slice. The times are simulated.
512 devices in a mesh: clip: 16 (over z), frame: 32 (over x, y, core).
Axes of the slice: x: 4, y: 4, z: 16, core: 2. Of those that a mesh axis runs over, the one named last changes fastest.
Arguments:
- tokens: bfloat16 [16, 32, 196, 1024], P('clip', 'frame'), may hold values from -6 to 6
- counts: int32 [16], P('clip'), may hold values from 1 to 32, 256 in all
- norm_gain: float32 [1024], replicated, may hold values from 0.1 to 1.9
- input_weights: bfloat16 [1024, 3072], P('frame', 'clip'), may hold values from -5 to 5
- output_weights: bfloat16 [1024, 1024], P('frame', 'clip'), may hold values from -0.1875 to 0.1875
- cotangent: bfloat16 [16, 32, 196, 1024], P('clip', 'frame'), may hold values from -6 to 6
Outputs:
- result: bfloat16 [16, 32, 196, 1024], P('clip', 'frame')
- grad_tokens: bfloat16 [16, 32, 196, 1024], P('clip', 'frame')
Inputs may be any that keep to these rules, and one draw needn't show every extreme that they name: The 16 counts sum to 256.
All inputs are finite; a program needn't handle non-finite values. No bound on the sum of `counts` on one device may be relied on, other than what follows from the above.
Results may differ from a plain program's by a relative error of at most 0.006.
Values may be sent and summed in bfloat16 or wider, within the bound.
A program may use at most 64 MiB of HBM per device.

v0:
```python
import jax
import jax.numpy as jnp
from jax import lax
from jax.sharding import PartitionSpec as P

DH = 64


EPSILON = 1e-06
NEGATIVE = -1e30


def joined_along(parts, dim):
    dims = list(parts.shape[1:])
    dims[dim] *= parts.shape[0]
    return jnp.moveaxis(parts, 0, dim).reshape(dims)


def gather_packed(arrays, axis, dims):
    ravelled = jnp.concatenate([a.reshape(-1) for a in arrays])
    lines, at, finished = (lax.all_gather(ravelled, axis), 0, [])
    for a, dim in zip(arrays, dims):
        parts = lines[:, at : at + a.size].reshape(-1, *a.shape)
        finished.append(joined_along(parts, dim))
        at += a.size
    return tuple(finished)


def sent_together(arrays, axis, dim, along):
    widths = [a.shape[along] for a in arrays]
    both = jnp.concatenate(arrays, axis=along)
    result = lax.all_gather(both, axis, axis=dim, tiled=True)
    return tuple(jnp.split(result, [sum(widths[:k]) for k in range(1, len(widths))], axis=along))


def in_one_piece(arrays, axis, split_dim, concat_dim, along):
    ends, at = ([], 0)
    for a in arrays[:-1]:
        at += a.shape[along]
        ends.append(at)
    both = jnp.concatenate(arrays, axis=along)
    return tuple(
        jnp.split(
            lax.all_to_all(both, axis, split_axis=split_dim, concat_axis=concat_dim, tiled=True),
            ends,
            axis=along,
        )
    )


def layer_norm(wide_precision_rows, norm_gain):
    average = jnp.mean(wide_precision_rows, axis=-1, keepdims=True)
    centred = wide_precision_rows - average
    variance = jnp.mean(centred * centred, axis=-1, keepdims=True)
    return centred * lax.rsqrt(variance + EPSILON) * norm_gain


def to_items(source):
    slot_count, patches, embedding_width = source.shape
    pair_count = embedding_width // (2 * DH)
    shaped = source.reshape(slot_count, 4, patches // 4, pair_count, 2 * DH)
    return shaped.transpose(0, 1, 3, 2, 4).reshape(slot_count, 4 * pair_count, patches // 4, 2 * DH)


def from_items(source):
    slot_count, item_count, quarter, pair_width = source.shape
    pair_count = item_count // 4
    shaped = source.reshape(slot_count, 4, pair_count, quarter, pair_width)
    return shaped.transpose(0, 1, 3, 2, 4).reshape(slot_count, 4 * quarter, pair_count * pair_width)


def split_heads(source):
    return source.reshape(source.shape[:3] + (2, DH))


def attention_probs(query_heads, key_heads, length):
    frames_total = query_heads.shape[0]
    scores = jnp.einsum(
        "tiphd,uiphd->iphtu", query_heads, key_heads, preferred_element_type=jnp.float32
    ) * DH ** (-0.5)
    live_keys = jnp.arange(frames_total) < length
    scores = jnp.where(live_keys, scores, NEGATIVE)
    highest = jnp.max(scores, axis=-1, keepdims=True)
    expanded = jnp.exp(scores - highest)
    return expanded / jnp.sum(expanded, axis=-1, keepdims=True)


def product(source, weights, pattern, out_width):
    flat_rows = source.reshape(-1, source.shape[-1])
    joined = jnp.einsum(pattern, flat_rows, weights, preferred_element_type=jnp.float32)
    return joined.reshape(source.shape[0], source.shape[1], out_width)


def per_device(tokens, counts, norm_gain, input_weights, output_weights, cotangent):
    columns_input, columns_output = gather_packed((input_weights, output_weights), "clip", (1, 1))
    whole_input, whole_output = sent_together((columns_input, columns_output), "frame", 0, 1)
    slot_count = tokens.shape[1]
    embedding_width = tokens.shape[3]
    length = counts[0]
    position = lax.axis_index("frame") * slot_count + jnp.arange(slot_count)
    occupied_frame_slots = position < length
    frame_presence_mask = occupied_frame_slots.astype(jnp.float32)[:, None, None]
    wide_precision_rows = tokens[0].astype(jnp.float32)
    normed = layer_norm(wide_precision_rows, norm_gain).astype(jnp.bfloat16)
    projected = product(normed, whole_input, "pk,kn->pn", 3 * embedding_width).astype(jnp.bfloat16)
    query_items, key_items, value_items = in_one_piece(
        (
            to_items(projected[..., :embedding_width]),
            to_items(projected[..., embedding_width : 2 * embedding_width]),
            to_items(projected[..., 2 * embedding_width :]),
        ),
        "frame",
        1,
        0,
        2,
    )
    query_heads = split_heads(query_items)
    key_heads = split_heads(key_items)
    value_heads = split_heads(value_items)
    probabilities = attention_probs(query_heads, key_heads, length)
    probs_low = probabilities.astype(jnp.bfloat16)
    attended = jnp.einsum(
        "iphtu,uiphd->tiphd", probs_low, value_heads, preferred_element_type=jnp.float32
    ).astype(jnp.bfloat16)
    item_shape = query_items.shape
    returned = lax.all_to_all(
        attended.reshape(item_shape), "frame", split_axis=0, concat_axis=1, tiled=True
    )
    attended_rows = from_items(returned)
    temporal_mixed_rows = product(attended_rows, whole_output, "pk,kn->pn", embedding_width)
    result = (wide_precision_rows + frame_presence_mask * temporal_mixed_rows).astype(jnp.bfloat16)
    wide_precision_cotangent = cotangent[0].astype(jnp.float32)
    output_gradient = (wide_precision_cotangent * frame_presence_mask).astype(jnp.bfloat16)
    grad_attended = product(output_gradient, whole_output, "pk,nk->pn", embedding_width).astype(
        jnp.bfloat16
    )
    grad_items = lax.all_to_all(
        to_items(grad_attended), "frame", split_axis=1, concat_axis=0, tiled=True
    )
    grad_heads = split_heads(grad_items)
    grad_probs = jnp.einsum(
        "tiphd,uiphd->iphtu", grad_heads, value_heads, preferred_element_type=jnp.float32
    )
    row_delta = jnp.einsum(
        "tiphd,tiphd->ipht", grad_heads, attended, preferred_element_type=jnp.float32
    )
    grad_scores = (probabilities * (grad_probs - row_delta[..., None])).astype(jnp.bfloat16)
    score_scale = DH ** (-0.5)
    grad_query = (
        jnp.einsum("iphtu,uiphd->tiphd", grad_scores, key_heads, preferred_element_type=jnp.float32)
        * score_scale
    ).astype(jnp.bfloat16)
    grad_keys = (
        jnp.einsum(
            "iphtu,tiphd->uiphd", grad_scores, query_heads, preferred_element_type=jnp.float32
        )
        * score_scale
    ).astype(jnp.bfloat16)
    grad_values = jnp.einsum(
        "iphtu,tiphd->uiphd", probs_low, grad_heads, preferred_element_type=jnp.float32
    ).astype(jnp.bfloat16)
    returned_grads = in_one_piece(
        (
            grad_query.reshape(item_shape),
            grad_keys.reshape(item_shape),
            grad_values.reshape(item_shape),
        ),
        "frame",
        0,
        1,
        2,
    )
    grad_projected = jnp.concatenate(
        [from_items(returned_piece) for returned_piece in returned_grads], axis=-1
    )
    grad_normed = product(grad_projected, whole_input, "pk,nk->pn", embedding_width)
    pullback = jax.vjp(lambda source: layer_norm(source, norm_gain), wide_precision_rows)[1]
    grad_rows = pullback(grad_normed)[0]
    grad_tokens = (wide_precision_cotangent + grad_rows).astype(jnp.bfloat16)
    return (result[None], grad_tokens[None])


def solution(mesh):
    in_specs = (
        P("clip", "frame", None, None),
        P("clip"),
        P(),
        P("frame", "clip"),
        P("frame", "clip"),
        P("clip", "frame", None, None),
    )
    out_specs = (P("clip", "frame", None, None), P("clip", "frame", None, None))
    return jax.shard_map(
        per_device, mesh=mesh, in_specs=in_specs, out_specs=out_specs, check_vma=False
    )
```

profile of v0, /device:TPU:25, one launch (start us, length us, event | category | flops | bytes accessed | tf_op | source)
XLA Modules:
  0.0 230.9 jit_solution(5391214955449037302)
XLA Ops:
  7.2 0.8 reshape.337
  8.0 0.8 reshape.336
  8.8 29.6 %all-gather = bf16[131072]{0:T(1024)(128)(2,1)S(1)} all-gather(bf16[8192]{0:T(1024)(128)(2,1)S(1)} %pad_maximum_fusion.3), channel_id=2, replica_groups=mesh['clip'=16,'frame'=32] {'clip'}, dimensions={0}, use_global_device_ids=true | all-gather | bytes 278528 | tf_op jit(solution)/shard_map/all_gather | solution.py:21
  38.5 0.1 reshape.370
  38.6 0.3 reshape.338
  39.0 0.2 copy.59
  39.1 0.3 reshape.339
  39.4 0.2 reshape.340
  39.6 0.1 reshape.341
  39.8 0.7 pad_maximum_fusion.2
  41.2 0.1 convert_reduce_fusion
  41.3 0.3 fusion.52
  41.6 70.4 %all-gather.3.cloned.1.call-done = bf16[1024,4096]{1,0:T(8,128)(2,1)} async-done(((bf16[32,4096]{1,0:T(8,128)(2,1)}), bf16[1024,4096]{1,0:T(8,128)(2,1)}) %all-gather.3.cloned.1.call-update) | async-done | bytes 8388624 | tf_op jit(solution)/shard_map/all_gather | solution.py:32
  111.9 2.4 %fusion.31 = bf16[196,1024]{1,0:T(8,128)(2,1)S(1)} fusion(bf16[1024,4096]{1,0:T(8,128)(2,1)} %all-gather.3.cloned.1.call-done, bf16[1,1,196,1024]{3,2,1,0:T(8,128)(2,1)S(1)} %copy-done.8, f32[]{:T(128)} %bitcast.4), kind=kOutput, calls=%fused_computation.28 | convolution fusion | flops 411844608 | bytes 2900480 | tf_op jit(solution)/shard_map/pk,nk->pn/dot_general | solution.py:90
  114.4 0.1 copy.113
  114.5 0.1 copy.151
  114.6 1.0 copy.76
  115.5 5.8 %all-to-all-start.2 = ((bf16[1,32,49,128]{3,2,0,1:T(8,128)(2,1)}), bf16[1,32,49,128]{3,2,0,1:T(8,128)(2,1)S(1)}, u32[]{:S(2)}, u32[]{:S(2)}) async-start(bf16[1,32,49,128]{3,2,0,1:T(8,128)(2,1)} %copy.76), calls=%async_computation.2 | async-start | bytes 917504 | tf_op jit(solution)/shard_map/all_to_all | solution.py:137
  121.4 4.3 %fusion.8 = bf16[1,196,3072]{2,1,0:T(8,128)(2,1)S(1)} fusion(bf16[1024,4096]{1,0:T(8,128)(2,1)} %all-gather.3.cloned.1.call-done, bf16[1,1,196,1024]{3,2,1,0:T(8,128)(2,1)S(1)} %copy-done, f32[1024]{0:T(1024)S(1)} %copy-done.10, f32[196]{0:T(256)S(1)} %fusion.70, f32[196]{0:T(256)S(1)} %broadcast_multiply_fusion), kind=kOutput, calls=%fused_computation.6 | convolution fusion | flops 1234731008 | bytes 7902752 | tf_op jit(solution)/shard_map/pk,kn->pn/dot_general | solution.py:90
  125.7 0.1 fusion.81
  125.8 0.1 copy.109
  126.0 0.1 copy.152
  126.0 0.1 copy.111
  126.2 0.1 copy.110
  126.3 0.1 copy_bitcast_fusion.4
  126.4 0.1 pad_maximum_fusion
  126.6 1.5 copy.64
  128.1 2.7 %all-to-all-done.2 = bf16[1,32,49,128]{3,2,0,1:T(8,128)(2,1)S(1)} async-done(((bf16[1,32,49,128]{3,2,0,1:T(8,128)(2,1)}), bf16[1,32,49,128]{3,2,0,1:T(8,128)(2,1)S(1)}, u32[]{:S(2)}, u32[]{:S(2)}) %all-to-all-start.2) | async-done | bytes 401440 | tf_op jit(solution)/shard_map/all_to_all | solution.py:137
  130.8 5.2 %all-to-all-start = ((bf16[1,32,147,128]{3,2,0,1:T(8,128)(2,1)}), bf16[1,32,147,128]{3,2,0,1:T(8,128)(2,1)S(1)}, u32[]{:S(2)}, u32[]{:S(2)}) async-start(bf16[1,32,147,128]{3,2,0,1:T(8,128)(2,1)} %copy.64), calls=%async_computation | async-start | bytes 2490368 | tf_op jit(solution)/shard_map/all_to_all | solution.py:44
  136.0 0.3 reshape.355
  136.4 1.8 bitcast_convert_fusion
  138.2 15.3 %all-to-all-done = bf16[1,32,147,128]{3,2,0,1:T(8,128)(2,1)S(1)} async-done(((bf16[1,32,147,128]{3,2,0,1:T(8,128)(2,1)}), bf16[1,32,147,128]{3,2,0,1:T(8,128)(2,1)S(1)}, u32[]{:S(2)}, u32[]{:S(2)}) %all-to-all-start) | async-done | bytes 1204256 | tf_op jit(solution)/shard_map/all_to_all | solution.py:44
  153.5 1.2 fusion.80
  154.7 2.2 reshape.376
  156.9 2.2 reshape.377
  159.0 1.3 reshape.375
  160.3 2.0 exponential_reduce_fusion
  162.3 2.9 %fusion.22 = bf16[32,1,49,2,64]{4,0,3,2,1:T(8,128)(2,1)} fusion(bf16[32,49,2,64]{3,2,0,1:T(2,128)(2,1)S(1)} %reshape.355, f32[49,2,32]{2,1,0:T(2,128)S(1)} %get-tuple-element.11, f32[49,2,32,32]{2,3,1,0:T(8,128)} %get-tuple-element.12), kind=kOutput, calls=%fused_computation.23 | convolution fusion | flops 13246464 | bytes 1216768 | tf_op jit(solution)/shard_map/iphtu,tiphd->uiphd/dot_general | solution.py:159
  165.2 1.0 multiply_reduce_fusion
  166.2 1.5 multiply_convert_fusion.2
  167.8 1.5 copy.101
  169.3 2.9 %reshape.374 = bf16[32,1,49,128]{3,2,1,0:T(8,128)(2,1)} reshape(bf16[32,1,49,2,64]{4,3,2,0,1:T(2,128)(2,1)} %copy.101) | data formatting | bytes 802816 | tf_op jit(solution)/shard_map/reshape | solution.py:127
  172.2 5.4 %all-to-all-start.1 = ((bf16[32,1,49,128]{3,2,1,0:T(8,128)(2,1)}), bf16[32,1,49,128]{3,2,1,0:T(8,128)(2,1)S(1)}, u32[]{:S(2)}, u32[]{:S(2)}) async-start(bf16[32,1,49,128]{3,2,1,0:T(8,128)(2,1)} %reshape.374), calls=%async_computation.1 | async-start | bytes 917504 | tf_op jit(solution)/shard_map/all_to_all | solution.py:126
  177.6 1.4 fusion.23
  179.0 1.7 copy.87
  180.7 2.8 %reshape.359 = bf16[32,1,49,128]{3,0,2,1:T(8,128)(2,1)} reshape(bf16[32,1,49,2,64]{4,3,0,2,1:T(2,128)(2,1)} %copy.87) | data formatting | bytes 802816 | tf_op jit(solution)/shard_map/reshape | solution.py:166
  183.5 1.7 copy.83
  185.2 2.8 %reshape.357 = bf16[32,1,49,128]{3,0,2,1:T(8,128)(2,1)} reshape(bf16[32,1,49,2,64]{4,3,0,2,1:T(2,128)(2,1)} %copy.83) | data formatting | bytes 802816 | tf_op jit(solution)/shard_map/reshape | solution.py:164
  188.0 0.4 fusion.24
  188.4 0.8 copy.85
  189.2 0.4 reshape.358
  189.5 0.1 pad_maximum_fusion.1
  189.7 1.6 copy.88
  191.3 7.5 %all-to-all-start.3 = ((bf16[32,1,147,128]{3,2,1,0:T(8,128)(2,1)}), bf16[32,1,147,128]{3,2,1,0:T(8,128)(2,1)S(1)}, u32[]{:S(2)}, u32[]{:S(2)}) async-start(bf16[32,1,147,128]{3,2,1,0:T(8,128)(2,1)} %copy.88), calls=%async_computation.3 | async-start | bytes 2490368 | tf_op jit(solution)/shard_map/all_to_all | solution.py:44
  198.9 0.1 copy.112
  198.9 3.0 %fusion.38 = bf16[1,1,196,1024]{3,2,1,0:T(8,128)(2,1)} fusion(bf16[196,1024]{1,0:T(8,128)(2,1)S(1)} %bitcast.190, bf16[1024,4096]{1,0:T(8,128)(2,1)} %all-gather.3.cloned.1.call-done, bf16[1,1,196,1024]{3,2,1,0:T(8,128)(2,1)S(1)} %copy-done, f32[]{:T(128)} %bitcast.4), kind=kOutput, calls=%fused_computation.38 | convolution fusion | flops 411844608 | bytes 3301888 | tf_op jit(solution)/shard_map/pk,kn->pn/dot_general | solution.py:90
  201.9 14.4 %all-to-all-done.3 = bf16[32,1,147,128]{3,2,1,0:T(8,128)(2,1)S(1)} async-done(((bf16[32,1,147,128]{3,2,1,0:T(8,128)(2,1)}), bf16[32,1,147,128]{3,2,1,0:T(8,128)(2,1)S(1)}, u32[]{:S(2)}, u32[]{:S(2)}) %all-to-all-start.3) | async-done | bytes 1204256 | tf_op jit(solution)/shard_map/all_to_all | solution.py:44
  216.3 0.4 fusion.79
  216.8 0.2 reshape.365
  217.0 0.2 reshape.361
  217.3 0.2 reshape.363
  217.5 5.1 %fusion.49 = (f32[196]{0:T(256)S(1)}, f32[196,1024]{1,0:T(8,128)S(1)}) fusion(bf16[1,1,196,1024]{3,2,1,0:T(8,128)(2,1)S(1)} %copy-done, f32[196]{0:T(256)S(1)} %broadcast_multiply_fusion, f32[1024]{0:T(1024)S(1)} %copy-done.10, bf16[1024,4096]{1,0:T(8,128)(2,1)} %all-gather.3.cloned.1.call-done, bf16[1,196,1024]{2,1,0:T(8,128)(2,1)S(1)} %reshape.365, ...), kind=kOutput, calls=%fused_computation.51 | convolution fusion | flops 1237741312 | bytes 8705568 | tf_op jit(solution)/shard_map/pk,nk->pn/dot_general | solution.py:90
  222.6 0.4 fusion.76
  223.0 1.1 fusion.63
  (46 shorter events, 0.7 us)
Async XLA Ops:
  7.2 104.8 %all-gather.3.cloned.1.call-start = ((), (), s32[]{:S(2)}) async-start(), calls=%async_computation.4 | async-start | bytes 8650752 | tf_op jit(solution)/shard_map/all_gather | solution.py:32
  38.6 2.6 %copy-start = (bf16[1,1,196,1024]{3,2,1,0:T(8,128)(2,1)S(1)}, bf16[1,1,196,1024]{3,2,1,0:T(8,128)(2,1)}, u32[]{:S(2)}) copy-start(bf16[1,1,196,1024]{3,2,1,0:T(8,128)(2,1)} %param.6) | copy-start | bytes 1204228
  38.9 73.0 %copy-start.8 = (bf16[1,1,196,1024]{3,2,1,0:T(8,128)(2,1)S(1)}, bf16[1,1,196,1024]{3,2,1,0:T(8,128)(2,1)}, u32[]{:S(2)}) copy-start(bf16[1,1,196,1024]{3,2,1,0:T(8,128)(2,1)} %param.11) | copy-start | bytes 1204228
  114.4 6.9 %copy-start.10 = (f32[1024]{0:T(1024)S(1)}, f32[1024]{0:T(1024)}, u32[]{:S(2)}) copy-start(f32[1024]{0:T(1024)} %param.8) | copy-start | bytes 12292
  115.5 15.2 %all-to-all-start.2 = ((bf16[1,32,49,128]{3,2,0,1:T(8,128)(2,1)}), bf16[1,32,49,128]{3,2,0,1:T(8,128)(2,1)S(1)}, u32[]{:S(2)}, u32[]{:S(2)}) async-start(bf16[1,32,49,128]{3,2,0,1:T(8,128)(2,1)} %copy.76), calls=%async_computation.2 | async-start | bytes 917504 | tf_op jit(solution)/shard_map/all_to_all | solution.py:137
  130.8 22.7 %all-to-all-start = ((bf16[1,32,147,128]{3,2,0,1:T(8,128)(2,1)}), bf16[1,32,147,128]{3,2,0,1:T(8,128)(2,1)S(1)}, u32[]{:S(2)}, u32[]{:S(2)}) async-start(bf16[1,32,147,128]{3,2,0,1:T(8,128)(2,1)} %copy.64), calls=%async_computation | async-start | bytes 2490368 | tf_op jit(solution)/shard_map/all_to_all | solution.py:44
  162.3 2.9 %copy-start.5 = (f32[49,2,32,64]{3,1,2,0:T(2,128)S(1)}, f32[49,2,32,64]{3,1,2,0:T(2,128)}, u32[]{:S(2)}) copy-start(f32[49,2,32,64]{3,1,2,0:T(2,128)} %bitcast_convert_fusion) | copy-start | bytes 2408452
  162.3 2.9 %copy-start.7 = (bf16[32,49,2,64]{3,2,1,0:T(2,128)(2,1)S(1)}, bf16[32,49,2,64]{3,2,1,0:T(2,128)(2,1)}, u32[]{:S(2)}) copy-start(bf16[32,49,2,64]{3,2,1,0:T(2,128)(2,1)} %reshape.375) | copy-start | bytes 1204228
  162.3 2.9 %copy-start.11 = (f32[49,2,32,32]{2,3,1,0:T(8,128)S(1)}, f32[49,2,32,32]{2,3,1,0:T(8,128)}, u32[]{:S(2)}) copy-start(f32[49,2,32,32]{2,3,1,0:T(8,128)} %get-tuple-element.12) | copy-start | bytes 1204228
  167.8 9.8 %copy-start.1 = (bf16[49,2,32,32]{2,3,1,0:T(8,128)(2,1)S(1)}, bf16[49,2,32,32]{2,3,1,0:T(8,128)(2,1)}, u32[]{:S(2)}) copy-start(bf16[49,2,32,32]{2,3,1,0:T(8,128)(2,1)} %multiply_convert_fusion.2) | copy-start | bytes 602116
  172.2 19.1 %all-to-all-start.1 = ((bf16[32,1,49,128]{3,2,1,0:T(8,128)(2,1)}), bf16[32,1,49,128]{3,2,1,0:T(8,128)(2,1)S(1)}, u32[]{:S(2)}, u32[]{:S(2)}) async-start(bf16[32,1,49,128]{3,2,1,0:T(8,128)(2,1)} %reshape.374), calls=%async_computation.1 | async-start | bytes 917504 | tf_op jit(solution)/shard_map/all_to_all | solution.py:126
  177.6 1.4 copy-start.6
  179.0 4.5 %copy-start.2 = (bf16[32,1,49,2,64]{4,0,3,2,1:T(8,128)(2,1)S(1)}, bf16[32,1,49,2,64]{4,0,3,2,1:T(8,128)(2,1)}, u32[]{:S(2)}) copy-start(bf16[32,1,49,2,64]{4,0,3,2,1:T(8,128)(2,1)} %fusion.23) | copy-start | bytes 1204228
  188.3 1.2 copy-start.3
  188.4 1.2 copy-start.4
  191.3 25.0 %all-to-all-start.3 = ((bf16[32,1,147,128]{3,2,1,0:T(8,128)(2,1)}), bf16[32,1,147,128]{3,2,1,0:T(8,128)(2,1)S(1)}, u32[]{:S(2)}, u32[]{:S(2)}) async-start(bf16[32,1,147,128]{3,2,1,0:T(8,128)(2,1)} %copy.88), calls=%async_computation.3 | async-start | bytes 2490368 | tf_op jit(solution)/shard_map/all_to_all | solution.py:44
  217.5 5.5 %copy-start.9 = (bf16[1,1,196,1024]{3,2,1,0:T(8,128)(2,1)S(1)}, bf16[1,1,196,1024]{3,2,1,0:T(8,128)(2,1)}, u32[]{:S(2)}) copy-start(bf16[1,1,196,1024]{3,2,1,0:T(8,128)(2,1)} %param.11) | copy-start | bytes 1204228
Sparse Core Ops, SparseCore 0:
  40.6 71.2 all-gather.2
where the time goes:
time: 234 us; the launch traced here: 231 us
  waiting for transfers between devices  103 us (44%)
  local copies, waits for them, and re-layouts  30.6 us (13%)
  blocking collectives  29.6 us (13%)
  matrix products  24 us (10%)
  starting transfers between devices  23.9 us (10%)
  between operations  15.2 us (6%)
  other arithmetic  4.73 us (2%)
    all_gather x1, waiting for transfers between devices, sent_together(): result = lax.all_gather(both, axis, axis=dim, tiled=True)  70.4 us
    all_to_all x2, waiting for transfers between devices, in_one_piece(): lax.all_to_all(both, axis, split_axis=split_dim, concat_axis=concat_dim,...  29.7 us
    all_gather x1, blocking collectives, gather_packed(): lines, at, finished = (lax.all_gather(ravelled, axis), 0, [])  29.6 us
    dot_general x4, matrix products, product(): jnp.einsum(pattern, flat_rows, weights, preferred_element_type=jnp.float32)  14.8 us
    all_to_all x2, starting transfers between devices, in_one_piece(): lax.all_to_all(both, axis, split_axis=split_dim, concat_axis=concat_dim,...  12.6 us
    another operation x4, local copies, waits for them, and re-layouts  5.93 us
    all_to_all x1, starting transfers between devices, per_device(): lax.all_to_all(to_items(grad_attended), 'frame', split_axis=1, concat_axi...  5.83 us
    all_to_all x1, starting transfers between devices, per_device(): lax.all_to_all(attended.reshape(item_shape), 'frame', split_axis=0, conca...  5.42 us
  transfers between devices with their start and end apart: 5, of which 4 were waited for; matrix products, arithmetic and copies ran while one was open for 11% of the time, Pallas kernels for 0%

commit v1 on v0

v1 whole, which is shorter than its diff:
```python
import functools
import jax, jax.numpy as jnp
from jax import lax
from jax.experimental import pallas as pl
from jax.experimental.pallas import tpu as pltpu
from jax.sharding import PartitionSpec as P

F32, BF16 = jnp.float32, jnp.bfloat16
D = 1024
ROWS = 256


def nn(a, b):
    return lax.dot_general(a, b, (((1,), (0,)), ((), ())), preferred_element_type=F32)


def nt(a, b):
    return lax.dot_general(a, b, (((1,), (1,)), ((), ())), preferred_element_type=F32)


def norm_stage(t_ref, nrm, xhat, rstd, gain_ref):
    def body(i, _):
        s = pl.ds(pl.multiple_of(i * 32, 32), 32)
        x = t_ref[pl.ds(i * 4, 4), 0].astype(F32).reshape(32, D)
        c = x - jnp.mean(x, axis=-1, keepdims=True)
        r = lax.rsqrt(jnp.mean(c * c, axis=-1, keepdims=True) + 1e-6)
        h = c * r
        xhat[s, :] = h
        rstd[s, :] = jnp.broadcast_to(r, (32, 128))
        nrm[s, :] = (h * gain_ref[...]).astype(BF16)
        return 0
    lax.fori_loop(0, 8, body, 0)


def mask_stage(cnt, t_ref, g, bias):
    def body(i, _):
        s = pl.ds(pl.multiple_of(i * 32, 32), 32)
        x = t_ref[pl.ds(i * 4, 4), 1].astype(F32).reshape(32, D)
        row = i * 32 + lax.broadcasted_iota(jnp.int32, (32, 1), 0)
        g[s, :] = (x * (row // 8 < cnt).astype(F32)).astype(BF16)
        u = i * 32 + lax.broadcasted_iota(jnp.int32, (32, ROWS), 0)
        t = lax.broadcasted_iota(jnp.int32, (32, ROWS), 1)
        ok = (u % 8 == t % 8) & (u // 8 < cnt)
        bias[s, :] = jnp.where(ok, 0.0, -1e30)
        return 0
    lax.fori_loop(0, 8, body, 0)


def attention_stage(proj, ga, att, dproj, bias):
    lane = lax.broadcasted_iota(jnp.int32, (ROWS, 128), 1) < 64
    eye = (lax.broadcasted_iota(jnp.int32, (128, 128), 0) == lax.broadcasted_iota(jnp.int32, (128, 128), 1)).astype(BF16)
    eye2 = (lax.broadcasted_iota(jnp.int32, (256, 256), 0) == lax.broadcasted_iota(jnp.int32, (256, 256), 1)).astype(BF16)
    top = lax.broadcasted_iota(jnp.int32, (128, ROWS), 0) < 64
    zero = jnp.zeros((ROWS, 128), BF16)

    def body(i, _):
        at = pl.multiple_of(i * 128, 128)
        q2, k2, v2 = (proj[:, pl.ds(pl.multiple_of(at + j * D, 128), 128)] for j in range(3))
        g2 = ga[:, pl.ds(at, 128)]
        kt, vt, gt = (nt(eye, a).astype(BF16) for a in (k2, v2, g2))
        gt32 = gt.astype(F32)
        parts = []
        for h in range(2):
            own = lane if h == 0 else ~lane
            st = nt(k2, jnp.where(own, q2, zero)) * 0.125 + bias[...]
            e = jnp.exp(st - jnp.max(st, axis=0, keepdims=True))
            p = e / jnp.sum(e, axis=0, keepdims=True)
            pb = p.astype(BF16)
            at_t = nn(vt, pb).astype(BF16)
            prod = gt32 * at_t.astype(F32)
            delta = jnp.sum(prod[h * 64:h * 64 + 64], axis=0, keepdims=True)
            ds = (p * (nt(v2, jnp.where(own, g2, zero)) - delta)).astype(BF16)
            parts.append((at_t, (nn(kt, ds) * 0.125).astype(BF16), nn(ds, q2) * 0.125, nn(pb, g2)))
        a, b = parts
        att[:, pl.ds(at, 128)] = nt(eye2, jnp.where(top, a[0], b[0])).astype(BF16)
        dproj[:, pl.ds(at, 128)] = nt(eye2, jnp.where(top, a[1], b[1])).astype(BF16)
        dproj[:, pl.ds(pl.multiple_of(at + D, 128), 128)] = jnp.where(lane, a[2], b[2]).astype(BF16)
        dproj[:, pl.ds(pl.multiple_of(at + 2 * D, 128), 128)] = jnp.where(lane, a[3], b[3]).astype(BF16)
        return 0
    lax.fori_loop(0, 8, body, 0)


def project_stage(nrm, w_ref, proj):
    def body(n, _):
        c = pl.ds(pl.multiple_of(n * 512, 512), 512)
        proj[:, c] = nn(nrm[...], w_ref[:, c]).astype(BF16)
        return 0
    lax.fori_loop(0, 6, body, 0)


def grad_attended_stage(g, w_ref, ga):
    def body(n, _):
        c = pl.ds(pl.multiple_of(n * 256, 256), 256)
        ga[:, c] = nt(g[...], w_ref[c, 3 * D:4 * D]).astype(BF16)
        return 0
    lax.fori_loop(0, 4, body, 0)


def result_stage(cnt, t_ref, att, w_ref, out):
    live = (lax.broadcasted_iota(jnp.int32, (ROWS, 1), 0) // 8 < cnt).astype(F32)
    def body(n, _):
        c = pl.ds(pl.multiple_of(n * 256, 256), 256)
        m = nn(att[...], w_ref[:, pl.ds(pl.multiple_of(3 * D + n * 256, 256), 256)])
        x = t_ref[:, 0, :, c].astype(F32).reshape(ROWS, 256)
        out[:, 0, :, c] = (x + live * m).astype(BF16).reshape(32, 8, 256)
        return 0
    lax.fori_loop(0, 4, body, 0)


def grad_stage(t_ref, dproj, w_ref, xhat, rstd, gain_ref, gn, out):
    def body(n, _):
        c = pl.ds(pl.multiple_of(n * 256, 256), 256)
        gn[:, c] = nt(dproj[...], w_ref[c, 0:3 * D])
        return 0
    lax.fori_loop(0, 4, body, 0)

    def last(i, _):
        s = pl.ds(pl.multiple_of(i * 32, 32), 32)
        h = xhat[s, :]
        dy = gn[s, :] * gain_ref[...]
        a = jnp.mean(dy, axis=-1, keepdims=True)
        b = jnp.mean(dy * h, axis=-1, keepdims=True)
        dx = rstd[s, 0:1] * (dy - a - h * b)
        f = pl.ds(i * 4, 4)
        x = t_ref[f, 1].astype(F32).reshape(32, D)
        out[f, 1] = (x + dx).astype(BF16).reshape(4, 8, D)
        return 0
    lax.fori_loop(0, 8, last, 0)


SCRATCH = [
    pltpu.VMEM((ROWS, D), BF16),
    pltpu.VMEM((ROWS, D), F32),
    pltpu.VMEM((ROWS, 128), F32),
    pltpu.VMEM((ROWS, D), BF16),
    pltpu.VMEM((ROWS, ROWS), F32),
    pltpu.VMEM((ROWS, 3 * D), BF16),
    pltpu.VMEM((ROWS, D), BF16),
    pltpu.VMEM((ROWS, D), BF16),
    pltpu.VMEM((ROWS, 3 * D), BF16),
    pltpu.VMEM((ROWS, D), F32),
]


def k2(stages, cnt_ref, gain_ref, t_ref, w_ref, out, nrm, xhat, rstd, g, bias, proj, ga, att, dproj, gn):
    cnt = cnt_ref[0]
    if 'n' in stages: norm_stage(t_ref, nrm, xhat, rstd, gain_ref)
    if 'm' in stages: mask_stage(cnt, t_ref, g, bias)
    if 'p' in stages: project_stage(nrm, w_ref, proj)
    if 'g' in stages: grad_attended_stage(g, w_ref, ga)
    if 'a' in stages: attention_stage(proj, ga, att, dproj, bias)
    if 'r' in stages: result_stage(cnt, t_ref, att, w_ref, out)
    if 'd' in stages: grad_stage(t_ref, dproj, w_ref, xhat, rstd, gain_ref, gn, out)


def call_k2(counts, gain, t, w, stages="nmpgard"):
    vm = pl.BlockSpec(memory_space=pltpu.VMEM)
    return pl.pallas_call(
        functools.partial(k2, stages),
        out_shape=jax.ShapeDtypeStruct((32, 2, 8, D), BF16),
        in_specs=[pl.BlockSpec(memory_space=pltpu.SMEM), vm, vm, vm],
        out_specs=vm,
        scratch_shapes=SCRATCH,
        compiler_params=pltpu.CompilerParams(vmem_limit_bytes=56 << 20),
        name="work_" + stages,
    )(counts, gain.reshape(1, D), t, w)


MESH = pl.DeviceIdType.MESH
WORKERS = 25


def worker_of(f):
    chip, core = f // 2, f % 2
    return (1 - core) * chip + core * (16 + (13 * chip) % 16)


def spot_of(j):
    return (2 * j) if j < 16 else 2 * ((5 * (j - 16)) % 16) + 1


def greet(peers):
    barrier = pltpu.get_barrier_semaphore()
    for peer in peers:
        pl.semaphore_signal(barrier, inc=1, device_id=peer, device_id_type=MESH)
    pl.semaphore_wait(barrier, len(peers))


def gather_kernel(tok_ref, cot_ref, win_ref, wout_ref, t_ref, w_ref, xs, wz, wl,
                  tx_send, tx_recv, own_sem, z_send, z_recv, s_send, s_recv):
    c, f = lax.axis_index("clip"), lax.axis_index("frame")
    core = f % 2
    barrier = pltpu.get_barrier_semaphore()

    def hail(i, _):
        pl.semaphore_signal(barrier, inc=1, device_id=(c, (f + i) % 32), device_id_type=MESH)
        return 0
    lax.fori_loop(1, 32, hail, 0)
    zs = [(c + d) % 16 for d in (4, 12, 8, 1, 15, 2, 14)]
    for z in zs:
        pl.semaphore_signal(barrier, inc=1, device_id=(z, f), device_id_type=MESH)
    r, q = c % 4, c // 4
    wz[r, q, :, 0:192] = win_ref[...]
    wz[r, q, :, 192:256] = wout_ref[...]
    for src, at in ((tok_ref, 0), (cot_ref, 1)):
        xs[0:24, at] = src[0:192].reshape(24, 8, D)
        xs[24, at, 0:4] = src[192:196]
        xs[24, at, 4:8] = jnp.zeros((4, D), BF16)
    pl.semaphore_wait(barrier, 38)

    def far(k):
        return pltpu.make_async_remote_copy(
            src_ref=wz.at[r, q], dst_ref=wz.at[r, q], send_sem=z_send.at[k], recv_sem=z_recv.at[k],
            device_id=(zs[k], f), device_id_type=MESH)

    for k in range(3):
        far(k).start()

    def tx(i):
        peer = (f + i) % 32
        j = worker_of(peer)
        return j, pltpu.make_async_remote_copy(
            src_ref=xs.at[jnp.minimum(j, WORKERS - 1)], dst_ref=t_ref.at[f], send_sem=tx_send.at[i], recv_sem=tx_recv.at[i],
            device_id=(c, peer), device_id_type=MESH)

    mine = worker_of(f)

    def tx_start(i, _):
        j, copy = tx(i)

        @pl.when(j < WORKERS)
        def _():
            copy.start()
        return 0
    lax.fori_loop(1, 32, tx_start, 0)
    own = pltpu.make_async_copy(xs.at[jnp.minimum(mine, WORKERS - 1)], t_ref.at[f], own_sem)
    own.start()

    for k in range(3):
        far(k).wait_recv()

    def near(k):
        return pltpu.make_async_remote_copy(
            src_ref=wz.at[r], dst_ref=wz.at[r], send_sem=z_send.at[k], recv_sem=z_recv.at[k],
            device_id=(zs[k], f), device_id_type=MESH)

    for k in range(3, 6):
        near(k).start()
    for k in range(3, 6):
        near(k).wait_recv()

    low = lax.broadcasted_iota(jnp.int32, (32, 128), 1) < 64
    for m in range(8):
        pair = []
        for z in (2 * m, 2 * m + 1):
            for h in range(2):
                pair.append(wz[z % 4, z // 4, :, 128 * h:128 * h + 128].astype(F32))
        a0, a1, b0, b1 = pair
        turned = pltpu.roll(b0, 64, 1)
        w_ref[f, :, 384 * m:384 * m + 128] = a0.astype(BF16)
        w_ref[f, :, 384 * m + 128:384 * m + 256] = jnp.where(low, a1, turned).astype(BF16)
        w_ref[f, :, 384 * m + 256:384 * m + 384] = jnp.where(low, turned, pltpu.roll(b1, 64, 1)).astype(BF16)
        w_ref[f, :, 3 * D + 128 * m:3 * D + 128 * m + 128] = jnp.where(low, pltpu.roll(a1, 64, 1), b1).astype(BF16)

    s1, s2 = 8 - 6 * core, 2 + 6 * core
    x, y = f // 8, (f // 2) % 4
    a = x * (1 - core) + y * core
    b = y * (1 - core) + x * core

    def spot(da, db):
        return ((a + da) % 4) * s1 + ((b + db) % 4) * s2 + core

    sent = []

    def send(block, to, sem, half=None):
        ref = w_ref.at[block] if half is None else w_ref.at[block, pl.ds(16 * half, 16)]
        copy = pltpu.make_async_remote_copy(
            src_ref=ref, dst_ref=ref, send_sem=s_send.at[len(sent)], recv_sem=s_recv.at[sem],
            device_id=(c, to), device_id_type=MESH)
        copy.start()
        sent.append(copy)

    def take(block, sem, half=None):
        ref = w_ref.at[block] if half is None else w_ref.at[block, pl.ds(16 * half, 16)]
        pltpu.make_async_remote_copy(
            src_ref=ref, dst_ref=ref, send_sem=s_send.at[0], recv_sem=s_recv.at[sem],
            device_id=(c, f), device_id_type=MESH).wait_recv()

    twin = f + 1 - 2 * core
    an, ap, bn, bp = spot(-1, 0), spot(1, 0), spot(0, -1), spot(0, 1)
    row = (0, -1, 1, 2)

    def along_b(n):
        send(spot(row[n], 0), bp, 4 + 4 * n)
        send(spot(row[n], 0), bn, 4 + 4 * n + 1)

    send(f, ap, 0)
    send(f, an, 1)
    along_b(0)
    send(f, twin, 20)
    take(an, 0)
    send(an, ap, 2, 0)
    along_b(1)
    send(an, twin, 21)
    take(ap, 1)
    send(ap, an, 3, 1)
    along_b(2)
    send(ap, twin, 22)
    take(spot(2, 0), 2, 0)
    take(spot(2, 0), 3, 1)
    along_b(3)
    send(spot(2, 0), twin, 23)
    for n in range(4):
        take(spot(row[n], -1), 4 + 4 * n)
        send(spot(row[n], -1), bp, 4 + 4 * n + 2, 0)
        send(spot(row[n], -1), twin, 24 + 3 * n)
        take(spot(row[n], 1), 4 + 4 * n + 1)
        send(spot(row[n], 1), bn, 4 + 4 * n + 3, 1)
        send(spot(row[n], 1), twin, 25 + 3 * n)
    for n in range(4):
        take(spot(row[n], 2), 4 + 4 * n + 2, 0)
        take(spot(row[n], 2), 4 + 4 * n + 3, 1)
        send(spot(row[n], 2), twin, 26 + 3 * n)
    def theirs(da, db):
        return ((b + da) % 4) * s2 + ((a + db) % 4) * s1 + 1 - core
    for n in range(4):
        take(theirs(row[n], 0), 20 + n)
    for n in range(4):
        for k, db in enumerate((-1, 1, 2)):
            take(theirs(row[n], db), 24 + 3 * n + k)

    @pl.when(mine < WORKERS)
    def _():
        def tx_wait(i, _):
            pltpu.make_async_remote_copy(
                src_ref=xs.at[0], dst_ref=t_ref.at[(f - i + 32) % 32], send_sem=tx_send.at[i], recv_sem=tx_recv.at[i],
                device_id=(c, f), device_id_type=MESH).wait_recv()
            return 0
        lax.fori_loop(1, 32, tx_wait, 0)
    own.wait()

    def tx_done(i, _):
        j, copy = tx(i)

        @pl.when(j < WORKERS)
        def _():
            copy.wait_send()
        return 0
    lax.fori_loop(1, 32, tx_done, 0)
    for k in range(3):
        far(k).wait_send()
        near(k + 3).wait_send()
    for copy in sent:
        copy.wait_send()


def return_kernel(y_ref, res_ref, grad_ref, z, send_sem, recv_sem, own_sem):
    c, f = lax.axis_index("clip"), lax.axis_index("frame")
    barrier = pltpu.get_barrier_semaphore()

    def hail(i, _):
        pl.semaphore_signal(barrier, inc=1, device_id=(c, (f + i) % 32), device_id_type=MESH)
        return 0
    lax.fori_loop(1, 32, hail, 0)
    pl.semaphore_wait(barrier, 31)
    mine = worker_of(f)
    slot = jnp.minimum(mine, WORKERS - 1)

    def copy(i):
        peer = (f + i) % 32
        return pltpu.make_async_remote_copy(
            src_ref=y_ref.at[peer], dst_ref=z.at[slot], send_sem=send_sem.at[i], recv_sem=recv_sem.at[i],
            device_id=(c, peer), device_id_type=MESH)

    own = pltpu.make_async_copy(y_ref.at[f], z.at[slot], own_sem)

    @pl.when(mine < WORKERS)
    def _():
        own.start()

        def start(i, _):
            copy(i).start()
            return 0
        lax.fori_loop(1, 32, start, 0)

    def wait(i, _):
        j = worker_of((f - i + 32) % 32)

        @pl.when(j < WORKERS)
        def _():
            pltpu.make_async_remote_copy(
                src_ref=y_ref.at[0], dst_ref=z.at[jnp.minimum(j, WORKERS - 1)], send_sem=send_sem.at[i], recv_sem=recv_sem.at[i],
                device_id=(c, f), device_id_type=MESH).wait_recv()
        return 0
    lax.fori_loop(1, 32, wait, 0)

    @pl.when(mine < WORKERS)
    def _():
        own.wait()

        def done(i, _):
            copy(i).wait_send()
            return 0
        lax.fori_loop(1, 32, done, 0)
    for ref, at in ((res_ref, 0), (grad_ref, 1)):
        ref[0:192] = z[0:24, at].reshape(192, D)
        ref[192:196] = z[24, at, 0:4]


VM = pl.BlockSpec(memory_space=pltpu.VMEM)


def per_device(tokens, counts, norm_gain, input_weights, output_weights, cotangent):
    dma = pltpu.SemaphoreType.DMA
    t, w = pl.pallas_call(
        gather_kernel,
        out_shape=(jax.ShapeDtypeStruct((32, 2, 8, D), BF16), jax.ShapeDtypeStruct((32, 32, 4 * D), BF16)),
        in_specs=[VM] * 4, out_specs=(VM, VM),
        scratch_shapes=[
            pltpu.VMEM((WORKERS, 2, 8, D), BF16), pltpu.VMEM((4, 4, 32, 256), BF16), pltpu.VMEM((8, 128), F32),
            dma((32,)), dma((32,)), dma, dma((6,)), dma((6,)), dma((36,)), dma((36,))],
        compiler_params=pltpu.CompilerParams(collective_id=0, has_side_effects=True, vmem_limit_bytes=40 << 20),
        name="gather",
    )(tokens[0, 0], cotangent[0, 0], input_weights, output_weights)
    y = call_k2(counts, norm_gain, t, w.reshape(D, 4 * D))
    res, grad = pl.pallas_call(
        return_kernel,
        out_shape=(jax.ShapeDtypeStruct((196, D), BF16),) * 2,
        in_specs=[VM], out_specs=(VM, VM),
        scratch_shapes=[pltpu.VMEM((WORKERS, 2, 8, D), BF16), dma((32,)), dma((32,)), dma],
        compiler_params=pltpu.CompilerParams(collective_id=1, has_side_effects=True, vmem_limit_bytes=40 << 20),
        name="give_back",
    )(y)
    return res[None, None], grad[None, None]


def solution(mesh):
    rows = P("clip", "frame", None, None)
    return jax.shard_map(
        per_device, mesh=mesh,
        in_specs=(rows, P("clip"), P(), P("frame", "clip"), P("frame", "clip"), rows),
        out_specs=(rows, rows), check_vma=False)
```

time: 234 us -> 121 us (0.52); the launches traced: 231 us -> 121 us
  Pallas kernels: 0 us -> 109 us
  waiting for transfers between devices: 103 us -> 0 us
  blocking collectives: 29.6 us -> 0 us
  matrix products: 24 us -> 0 us
  starting transfers between devices: 23.9 us -> 0 us
  local copies, waits for them, and re-layouts: 30.6 us -> 10.4 us
  between operations: 15.2 us -> 1.32 us
  other arithmetic: 4.73 us -> 0 us
    pallas_call x0 -> x3, Pallas kernels: none -> 109 us  [the longest x1 57.6 us: per_device(): pl.pallas_call(gather_kernel, out_shape=(jax.ShapeDtypeStruct((32, 2, 8,...]
    all_gather x1 -> x0, waiting for transfers between devices: 70.4 us -> none  [sent_together(): result = lax.all_gather(both, axis, axis=dim, tiled=True)]
    all_to_all x4 -> x0, waiting for transfers between devices: 32.4 us -> none  [the longest x2 29.7 us: in_one_piece(): lax.all_to_all(both, axis, split_axis=split_dim, concat_axis=concat_dim,...]
    all_gather x1 -> x0, blocking collectives: 29.6 us -> none  [gather_packed(): lines, at, finished = (lax.all_gather(ravelled, axis), 0, [])]
    all_to_all x4 -> x0, starting transfers between devices: 23.9 us -> none  [the longest x2 12.6 us: in_one_piece(): lax.all_to_all(both, axis, split_axis=split_dim, concat_axis=concat_dim,...]
    dot_general x9 -> x0, matrix products: 22 us -> none  [the longest x4 14.8 us: product(): jnp.einsum(pattern, flat_rows, weights, preferred_element_type=jnp.float32)]
    reshape x22 -> x0, local copies, waits for them, and re-layouts: 14.8 us -> none  [the longest x2 4.37 us: per_device(): attended.reshape(item_shape)]
    unnamed x34 -> x16, local copies, waits for them, and re-layouts: 0.55 us -> 10.4 us
  transfers between devices with their start and end apart: 5 -> 0, of which waited for: 4 -> 0; matrix products, arithmetic and copies ran while one was open for 11% -> 0% of each run, Pallas kernels for 0% -> 0%
where the time goes in v1:
time: 121 us
  Pallas kernels  109 us (90%)
  local copies, waits for them, and re-layouts  10.4 us (9%)
  between operations  1.32 us (1%)
    pallas_call x1, Pallas kernels, per_device(): pl.pallas_call(gather_kernel, out_shape=(jax.ShapeDtypeStruct((32, 2, 8,...  57.6 us
    pallas_call x1, Pallas kernels, call_k2(): pl.pallas_call(functools.partial(k2, stages), out_shape=jax.ShapeDtypeStr...  28 us
    pallas_call x1, Pallas kernels, per_device(): pl.pallas_call(return_kernel, out_shape=(jax.ShapeDtypeStruct((196, D), B...  23.3 us
    unnamed x16, local copies, waits for them, and re-layouts  10.4 us

profile of v1, /device:TPU:25, one launch (start us, length us, event | category | flops | bytes accessed | tf_op | source)
XLA Modules:
  0.0 120.6 jit_solution(5089689421201185492)
XLA Ops:
  1.3 0.0 copy-start.3
  1.3 1.0 copy-done.3
  2.3 0.0 copy-start.4
  2.3 1.0 copy-done.4
  3.3 0.0 copy-start.5
  3.3 0.7 copy-done.5
  4.0 0.0 copy-start.6
  4.0 0.7 copy-done.6
  4.7 57.6 %gather.1 = (bf16[32,2,8,1024]{3,2,1,0:T(8,128)(2,1)S(1)}, bf16[32,32,4096]{2,1,0:T(8,128)(2,1)S(1)}) custom-call(bf16[196,1024]{1,0:T(8,128)(2,1)S(1)} %bitcast.7, bf16[196,1024]{1,0:T(8,128)(2,1)S(1)} %bitcast.8, bf16[32,192]{1,0:T(8,128)(2,1)S(1)} %copy-done.5, bf16[32,64]{1,0:T(8,128)(2,1)S(1)} %copy-done.6), custom_call_target="tpu_custom_call" | custom-call | tf_op jit(solution)/shard_map/gather/pallas_call | solution.py:415
  62.3 0.0 copy-start
  62.3 3.2 %copy-done = bf16[32,32,4096]{2,1,0:T(8,128)(2,1)} copy-done((bf16[32,32,4096]{2,1,0:T(8,128)(2,1)}, bf16[32,32,4096]{2,1,0:T(8,128)(2,1)S(1)}, u32[]{:S(2)}) %copy-start) | copy-done | bytes 8388632
  65.5 0.0 copy-start.2
  65.5 1.1 copy-done.2
  66.6 28.0 %work_nmpgard.1.y_ref = bf16[32,2,8,1024]{3,2,1,0:T(8,128)(2,1)} custom-call(s32[1]{0:T(128)S(6)} %copy.10.cnt_ref, f32[1,1024]{1,0:T(1,128)} %bitcast.11, bf16[32,2,8,1024]{3,2,1,0:T(8,128)(2,1)} %copy-done.2, bf16[1024,4096]{1,0:T(8,128)(2,1)} %bitcast.6), custom_call_target="tpu_custom_call" | custom-call | tf_op jit(solution)/shard_map/work_nmpgard/pallas_call | solution.py:158
  94.6 0.0 copy-start.1
  94.6 1.2 %copy-done.1 = bf16[32,2,8,1024]{3,2,1,0:T(8,128)(2,1)S(1)} copy-done((bf16[32,2,8,1024]{3,2,1,0:T(8,128)(2,1)S(1)}, bf16[32,2,8,1024]{3,2,1,0:T(8,128)(2,1)}, u32[]{:S(2)}) %copy-start.1) | copy-done | bytes 1048600
  95.8 23.3 %give_back.1 = (bf16[196,1024]{1,0:T(8,128)(2,1)S(1)}, bf16[196,1024]{1,0:T(8,128)(2,1)S(1)}) custom-call(bf16[32,2,8,1024]{3,2,1,0:T(8,128)(2,1)S(1)} %copy-done.1), custom_call_target="tpu_custom_call" | custom-call | tf_op jit(solution)/shard_map/give_back/pallas_call | solution.py:426
  119.1 0.8 copy.11
  119.8 0.8 copy.12
Async XLA Ops:
  1.3 1.0 copy-start.3
  2.3 1.0 copy-start.4
  3.3 0.7 copy-start.5
  4.0 0.7 copy-start.6
  62.3 3.2 %copy-start = (bf16[32,32,4096]{2,1,0:T(8,128)(2,1)}, bf16[32,32,4096]{2,1,0:T(8,128)(2,1)S(1)}, u32[]{:S(2)}) copy-start(bf16[32,32,4096]{2,1,0:T(8,128)(2,1)S(1)} %get-tuple-element.7) | copy-start | bytes 25165828
  65.5 1.1 copy-start.2
  94.6 1.2 %copy-start.1 = (bf16[32,2,8,1024]{3,2,1,0:T(8,128)(2,1)S(1)}, bf16[32,2,8,1024]{3,2,1,0:T(8,128)(2,1)}, u32[]{:S(2)}) copy-start(bf16[32,2,8,1024]{3,2,1,0:T(8,128)(2,1)} %work_nmpgard.1.y_ref) | copy-start | bytes 3145732

commit v2 on v1

--- a/solution.py
+++ b/solution.py
@@ -83,7 +83,7 @@
 def project_stage(nrm, w_ref, proj):
     def body(n, _):
         c = pl.ds(pl.multiple_of(n * 512, 512), 512)
-        proj[:, c] = nn(nrm[...], w_ref[:, c]).astype(BF16)
+        proj[:, c] = nn(nrm[...], w_ref[:, :, c].reshape(D, 512)).astype(BF16)
         return 0
     lax.fori_loop(0, 6, body, 0)
 
@@ -91,7 +91,7 @@
 def grad_attended_stage(g, w_ref, ga):
     def body(n, _):
         c = pl.ds(pl.multiple_of(n * 256, 256), 256)
-        ga[:, c] = nt(g[...], w_ref[c, 3 * D:4 * D]).astype(BF16)
+        ga[:, c] = nt(g[...], w_ref[pl.ds(n * 8, 8), :, 3 * D:4 * D].reshape(256, D)).astype(BF16)
         return 0
     lax.fori_loop(0, 4, body, 0)
 
@@ -100,7 +100,7 @@
     live = (lax.broadcasted_iota(jnp.int32, (ROWS, 1), 0) // 8 < cnt).astype(F32)
     def body(n, _):
         c = pl.ds(pl.multiple_of(n * 256, 256), 256)
-        m = nn(att[...], w_ref[:, pl.ds(pl.multiple_of(3 * D + n * 256, 256), 256)])
+        m = nn(att[...], w_ref[:, :, pl.ds(pl.multiple_of(3 * D + n * 256, 256), 256)].reshape(D, 256))
         x = t_ref[:, 0, :, c].astype(F32).reshape(ROWS, 256)
         out[:, 0, :, c] = (x + live * m).astype(BF16).reshape(32, 8, 256)
         return 0
@@ -110,7 +110,7 @@
 def grad_stage(t_ref, dproj, w_ref, xhat, rstd, gain_ref, gn, out):
     def body(n, _):
         c = pl.ds(pl.multiple_of(n * 256, 256), 256)
-        gn[:, c] = nt(dproj[...], w_ref[c, 0:3 * D])
+        gn[:, c] = nt(dproj[...], w_ref[pl.ds(n * 8, 8), :, 0:3 * D].reshape(256, 3 * D))
         return 0
     lax.fori_loop(0, 4, body, 0)
 
@@ -142,30 +142,6 @@
 ]
 
 
-def k2(stages, cnt_ref, gain_ref, t_ref, w_ref, out, nrm, xhat, rstd, g, bias, proj, ga, att, dproj, gn):
-    cnt = cnt_ref[0]
-    if 'n' in stages: norm_stage(t_ref, nrm, xhat, rstd, gain_ref)
-    if 'm' in stages: mask_stage(cnt, t_ref, g, bias)
-    if 'p' in stages: project_stage(nrm, w_ref, proj)
-    if 'g' in stages: grad_attended_stage(g, w_ref, ga)
-    if 'a' in stages: attention_stage(proj, ga, att, dproj, bias)
-    if 'r' in stages: result_stage(cnt, t_ref, att, w_ref, out)
-    if 'd' in stages: grad_stage(t_ref, dproj, w_ref, xhat, rstd, gain_ref, gn, out)
-
-
-def call_k2(counts, gain, t, w, stages="nmpgard"):
-    vm = pl.BlockSpec(memory_space=pltpu.VMEM)
-    return pl.pallas_call(
-        functools.partial(k2, stages),
-        out_shape=jax.ShapeDtypeStruct((32, 2, 8, D), BF16),
-        in_specs=[pl.BlockSpec(memory_space=pltpu.SMEM), vm, vm, vm],
-        out_specs=vm,
-        scratch_shapes=SCRATCH,
-        compiler_params=pltpu.CompilerParams(vmem_limit_bytes=56 << 20),
-        name="work_" + stages,
-    )(counts, gain.reshape(1, D), t, w)
-
-
 MESH = pl.DeviceIdType.MESH
 WORKERS = 25
 
@@ -179,17 +155,15 @@
     return (2 * j) if j < 16 else 2 * ((5 * (j - 16)) % 16) + 1
 
 
-def greet(peers):
-    barrier = pltpu.get_barrier_semaphore()
-    for peer in peers:
-        pl.semaphore_signal(barrier, inc=1, device_id=peer, device_id_type=MESH)
-    pl.semaphore_wait(barrier, len(peers))
-
-
-def gather_kernel(tok_ref, cot_ref, win_ref, wout_ref, t_ref, w_ref, xs, wz, wl,
-                  tx_send, tx_recv, own_sem, z_send, z_recv, s_send, s_recv):
+def block_kernel(cnt_ref, gain_ref, tok_hbm, cot_hbm, win_hbm, wout_hbm, res_ref, grad_ref,
+                 tok_ref, cot_ref, win_ref, wout_ref, xs, t_ref, y_ref, z_ref, wz, w_ref, work,
+                 in_sem, tx_send, tx_recv, own_sem, z_send, z_recv, s_send, s_recv, ry_send, ry_recv):
     c, f = lax.axis_index("clip"), lax.axis_index("frame")
     core = f % 2
+    loads = [pltpu.make_async_copy(src, dst, in_sem.at[k]) for k, (src, dst) in enumerate(
+        ((win_hbm, win_ref), (wout_hbm, wout_ref), (tok_hbm.at[0, 0], tok_ref), (cot_hbm.at[0, 0], cot_ref)))]
+    for load in loads:
+        load.start()
     barrier = pltpu.get_barrier_semaphore()
 
     def hail(i, _):
@@ -199,6 +173,8 @@
     zs = [(c + d) % 16 for d in (4, 12, 8, 1, 15, 2, 14)]
     for z in zs:
         pl.semaphore_signal(barrier, inc=1, device_id=(z, f), device_id_type=MESH)
+    for load in loads:
+        load.wait()
     r, q = c % 4, c // 4
     wz[r, q, :, 0:192] = win_ref[...]
     wz[r, q, :, 192:256] = wout_ref[...]
@@ -339,6 +315,63 @@
         lax.fori_loop(1, 32, tx_wait, 0)
     own.wait()
 
+
+    slot = jnp.minimum(mine, WORKERS - 1)
+
+    def back(i, part):
+        peer = (f + i) % 32
+        return pltpu.make_async_remote_copy(
+            src_ref=y_ref.at[peer, part], dst_ref=z_ref.at[part, slot], send_sem=ry_send.at[part, i],
+            recv_sem=ry_recv.at[part, i], device_id=(c, peer), device_id_type=MESH)
+
+    def give(part):
+        def start(i, _):
+            back(i, part).start()
+            return 0
+        pltpu.make_async_copy(y_ref.at[f, part], z_ref.at[part, slot], ry_send.at[part, 0]).start()
+        lax.fori_loop(1, 32, start, 0)
+
+    @pl.when(mine < WORKERS)
+    def _():
+        cnt = cnt_ref[0]
+        nrm, xhat, rstd, g, bias, proj, ga, att, dproj, gn = work
+        norm_stage(t_ref, nrm, xhat, rstd, gain_ref)
+        mask_stage(cnt, t_ref, g, bias)
+        project_stage(nrm, w_ref, proj)
+        grad_attended_stage(g, w_ref, ga)
+        attention_stage(proj, ga, att, dproj, bias)
+        result_stage(cnt, t_ref, att, w_ref, y_ref)
+        give(0)
+        grad_stage(t_ref, dproj, w_ref, xhat, rstd, gain_ref, gn, y_ref)
+        give(1)
+
+    for part, ref in ((0, res_ref), (1, grad_ref)):
+        def wait(i, _):
+            j = worker_of((f - i + 32) % 32)
+
+            @pl.when(j < WORKERS)
+            def _():
+                pltpu.make_async_remote_copy(
+                    src_ref=y_ref.at[0, part], dst_ref=z_ref.at[part, jnp.minimum(j, WORKERS - 1)],
+                    send_sem=ry_send.at[part, i], recv_sem=ry_recv.at[part, i],
+                    device_id=(c, f), device_id_type=MESH).wait_recv()
+            return 0
+        lax.fori_loop(1, 32, wait, 0)
+
+        @pl.when(mine < WORKERS)
+        def _():
+            pltpu.make_async_copy(y_ref.at[f, part], z_ref.at[part, slot], ry_send.at[part, 0]).wait()
+        ref[0, 0, 0:192] = z_ref[part, 0:24].reshape(192, D)
+        ref[0, 0, 192:196] = z_ref[part, 24, 0:4]
+
+    @pl.when(mine < WORKERS)
+    def _():
+        def back_done(i, _):
+            back(i, 0).wait_send()
+            back(i, 1).wait_send()
+            return 0
+        lax.fori_loop(1, 32, back_done, 0)
+
     def tx_done(i, _):
         j, copy = tx(i)
 
@@ -354,84 +387,23 @@
         copy.wait_send()
 
 
-def return_kernel(y_ref, res_ref, grad_ref, z, send_sem, recv_sem, own_sem):
-    c, f = lax.axis_index("clip"), lax.axis_index("frame")
-    barrier = pltpu.get_barrier_semaphore()
-
-    def hail(i, _):
-        pl.semaphore_signal(barrier, inc=1, device_id=(c, (f + i) % 32), device_id_type=MESH)
-        return 0
-    lax.fori_loop(1, 32, hail, 0)
-    pl.semaphore_wait(barrier, 31)
-    mine = worker_of(f)
-    slot = jnp.minimum(mine, WORKERS - 1)
-
-    def copy(i):
-        peer = (f + i) % 32
-        return pltpu.make_async_remote_copy(
-            src_ref=y_ref.at[peer], dst_ref=z.at[slot], send_sem=send_sem.at[i], recv_sem=recv_sem.at[i],
-            device_id=(c, peer), device_id_type=MESH)
-
-    own = pltpu.make_async_copy(y_ref.at[f], z.at[slot], own_sem)
-
-    @pl.when(mine < WORKERS)
-    def _():
-        own.start()
-
-        def start(i, _):
-            copy(i).start()
-            return 0
-        lax.fori_loop(1, 32, start, 0)
-
-    def wait(i, _):
-        j = worker_of((f - i + 32) % 32)
-
-        @pl.when(j < WORKERS)
-        def _():
-            pltpu.make_async_remote_copy(
-                src_ref=y_ref.at[0], dst_ref=z.at[jnp.minimum(j, WORKERS - 1)], send_sem=send_sem.at[i], recv_sem=recv_sem.at[i],
-                device_id=(c, f), device_id_type=MESH).wait_recv()
-        return 0
-    lax.fori_loop(1, 32, wait, 0)
-
-    @pl.when(mine < WORKERS)
-    def _():
-        own.wait()
-
-        def done(i, _):
-            copy(i).wait_send()
-            return 0
-        lax.fori_loop(1, 32, done, 0)
-    for ref, at in ((res_ref, 0), (grad_ref, 1)):
-        ref[0:192] = z[0:24, at].reshape(192, D)
-        ref[192:196] = z[24, at, 0:4]
-
-
-VM = pl.BlockSpec(memory_space=pltpu.VMEM)
-
-
 def per_device(tokens, counts, norm_gain, input_weights, output_weights, cotangent):
     dma = pltpu.SemaphoreType.DMA
-    t, w = pl.pallas_call(
-        gather_kernel,
-        out_shape=(jax.ShapeDtypeStruct((32, 2, 8, D), BF16), jax.ShapeDtypeStruct((32, 32, 4 * D), BF16)),
-        in_specs=[VM] * 4, out_specs=(VM, VM),
+    vm = pl.BlockSpec(memory_space=pltpu.VMEM)
+    hbm = pl.BlockSpec(memory_space=pl.ANY)
+    return tuple(pl.pallas_call(
+        block_kernel,
+        out_shape=(jax.ShapeDtypeStruct((1, 1, 196, D), BF16),) * 2,
+        in_specs=[pl.BlockSpec(memory_space=pltpu.SMEM), vm, hbm, hbm, hbm, hbm], out_specs=(vm, vm),
         scratch_shapes=[
-            pltpu.VMEM((WORKERS, 2, 8, D), BF16), pltpu.VMEM((4, 4, 32, 256), BF16), pltpu.VMEM((8, 128), F32),
-            dma((32,)), dma((32,)), dma, dma((6,)), dma((6,)), dma((36,)), dma((36,))],
-        compiler_params=pltpu.CompilerParams(collective_id=0, has_side_effects=True, vmem_limit_bytes=40 << 20),
-        name="gather",
-    )(tokens[0, 0], cotangent[0, 0], input_weights, output_weights)
-    y = call_k2(counts, norm_gain, t, w.reshape(D, 4 * D))
-    res, grad = pl.pallas_call(
-        return_kernel,
-        out_shape=(jax.ShapeDtypeStruct((196, D), BF16),) * 2,
-        in_specs=[VM], out_specs=(VM, VM),
-        scratch_shapes=[pltpu.VMEM((WORKERS, 2, 8, D), BF16), dma((32,)), dma((32,)), dma],
-        compiler_params=pltpu.CompilerParams(collective_id=1, has_side_effects=True, vmem_limit_bytes=40 << 20),
-        name="give_back",
-    )(y)
-    return res[None, None], grad[None, None]
+            pltpu.VMEM((196, D), BF16), pltpu.VMEM((196, D), BF16), pltpu.VMEM((32, 192), BF16), pltpu.VMEM((32, 64), BF16),
+            pltpu.VMEM((WORKERS, 2, 8, D), BF16), pltpu.VMEM((32, 2, 8, D), BF16), pltpu.VMEM((32, 2, 8, D), BF16),
+            pltpu.VMEM((2, WORKERS, 8, D), BF16), pltpu.VMEM((4, 4, 32, 256), BF16), pltpu.VMEM((32, 32, 4 * D), BF16),
+            SCRATCH,
+            dma((4,)), dma((32,)), dma((32,)), dma, dma((6,)), dma((6,)), dma((36,)), dma((36,)), dma((2, 32)), dma((2, 32))],
+        compiler_params=pltpu.CompilerParams(collective_id=0, has_side_effects=True, vmem_limit_bytes=56 << 20),
+        name="temporal_block",
+    )(counts, norm_gain.reshape(1, D), tokens, cotangent, input_weights, output_weights))
 
 
 def solution(mesh):

time: 121 us -> 100 us (0.83)
  Pallas kernels: 109 us -> 94.9 us
  local copies, waits for them, and re-layouts: 10.4 us -> 2.59 us
    pallas_call x3 -> x1, Pallas kernels: 109 us -> 94.9 us  [per_device(): pl.pallas_call(block_kernel, out_shape=(jax.ShapeDtypeStruct((1, 1, 196,...]
    unnamed x16 -> x4, local copies, waits for them, and re-layouts: 10.4 us -> 2.59 us
where the time goes in v2:
time: 100 us; the launch traced here: 98.8 us
  Pallas kernels  94.9 us (95%)
  local copies, waits for them, and re-layouts  2.59 us (3%)
  between operations  1.29 us (1%)
    pallas_call x1, Pallas kernels, per_device(): pl.pallas_call(block_kernel, out_shape=(jax.ShapeDtypeStruct((1, 1, 196,...  94.9 us
    unnamed x4, local copies, waits for them, and re-layouts  2.59 us

profile of v2, /device:TPU:25, one launch (start us, length us, event | category | flops | bytes accessed | tf_op | source)
XLA Modules:
  0.0 98.8 jit_solution(12569701862982974592)
XLA Ops:
  1.3 94.9 %temporal_block.1 = (bf16[1,1,196,1024]{3,2,1,0:T(8,128)(2,1)}, bf16[1,1,196,1024]{3,2,1,0:T(8,128)(2,1)}) custom-call(s32[1]{0:T(128)S(6)} %copy.10.cnt_ref, f32[1,1024]{1,0:T(1,128)} %bitcast.1, bf16[1,1,196,1024]{3,2,1,0:T(8,128)(2,1)} %tok_hbm.1, bf16[1,1,196,1024]{3,2,1,0:T(8,128)(2,1)} %cot_hbm.1, bf16[32,192]{1,0:T(8,128)(2,1)} %win_hbm.1, ...), custom_call_target="tpu_custom_call" | custom-call | tf_op jit(solution)/shard_map/temporal_block/pallas_call | solution.py:394
  96.2 0.0 copy-start
  96.2 1.8 %copy.11 = bf16[1,1,196,1024]{3,2,1,0:T(8,128)(2,1)} copy(bf16[1,1,196,1024]{3,2,1,0:T(8,128)(2,1)} %get-tuple-element.4) | data formatting | bytes 802816
  98.0 0.0 copy-done
  98.0 0.8 copy.12
Async XLA Ops:
  96.2 1.8 %copy-start = (bf16[1,1,196,1024]{3,2,1,0:T(8,128)(2,1)S(1)}, bf16[1,1,196,1024]{3,2,1,0:T(8,128)(2,1)}, u32[]{:S(2)}) copy-start(bf16[1,1,196,1024]{3,2,1,0:T(8,128)(2,1)} %get-tuple-element.5) | copy-start | bytes 1204228

commit v3 on v2

v3 whole, which is shorter than its diff:
```python
import functools
import jax, jax.numpy as jnp
from jax import lax
from jax.experimental import pallas as pl
from jax.experimental.pallas import tpu as pltpu
from jax.sharding import PartitionSpec as P

F32, BF16 = jnp.float32, jnp.bfloat16
D = 1024
ROWS = 256


def nn(a, b):
    return lax.dot_general(a, b, (((1,), (0,)), ((), ())), preferred_element_type=F32)


def nt(a, b):
    return lax.dot_general(a, b, (((1,), (1,)), ((), ())), preferred_element_type=F32)


def norm_stage(t_ref, nrm, xhat, rstd, gain_ref):
    def body(i, _):
        s = pl.ds(pl.multiple_of(i * 32, 32), 32)
        x = t_ref[pl.ds(i * 4, 4), 0].astype(F32).reshape(32, D)
        c = x - jnp.mean(x, axis=-1, keepdims=True)
        r = lax.rsqrt(jnp.mean(c * c, axis=-1, keepdims=True) + 1e-6)
        h = c * r
        xhat[s, :] = h
        rstd[s, :] = jnp.broadcast_to(r, (32, 128))
        nrm[s, :] = (h * gain_ref[...]).astype(BF16)
        return 0
    lax.fori_loop(0, 8, body, 0)


def mask_stage(cnt, t_ref, g, bias):
    def body(i, _):
        s = pl.ds(pl.multiple_of(i * 32, 32), 32)
        x = t_ref[pl.ds(i * 4, 4), 1].astype(F32).reshape(32, D)
        row = i * 32 + lax.broadcasted_iota(jnp.int32, (32, 1), 0)
        g[s, :] = (x * (row // 8 < cnt).astype(F32)).astype(BF16)
        u = i * 32 + lax.broadcasted_iota(jnp.int32, (32, ROWS), 0)
        t = lax.broadcasted_iota(jnp.int32, (32, ROWS), 1)
        ok = (u % 8 == t % 8) & (u // 8 < cnt)
        bias[s, :] = jnp.where(ok, 0.0, -1e30)
        return 0
    lax.fori_loop(0, 8, body, 0)


def attention_stage(proj, ga, att, dproj, bias):
    lane = lax.broadcasted_iota(jnp.int32, (ROWS, 128), 1) < 64
    top = lax.broadcasted_iota(jnp.int32, (128, ROWS), 0) < 64
    zero = jnp.zeros((ROWS, 128), BF16)
    eighth = jnp.asarray(0.125, BF16)

    def body(i, _):
        at = pl.multiple_of(i * 128, 128)
        q2, k2, v2 = (proj[:, pl.ds(pl.multiple_of(at + j * D, 128), 128)] for j in range(3))
        q2 = q2 * eighth
        g2 = ga[:, pl.ds(at, 128)]
        kt, vt, gt = k2.T * eighth, v2.T, g2.T.astype(F32)
        own = (lane, ~lane)
        st = [nt(k2, jnp.where(own[h], q2, zero)) for h in range(2)]
        dp = [nt(v2, jnp.where(own[h], g2, zero)) for h in range(2)]
        p, pb, at_t, ds = [], [], [], []
        for h in range(2):
            s = st[h] + bias[...]
            e = jnp.exp(s - jnp.max(s, axis=0, keepdims=True))
            p.append(e * (1.0 / jnp.sum(e, axis=0, keepdims=True)))
            pb.append(p[h].astype(BF16))
        for h in range(2):
            at_t.append(nn(vt, pb[h]).astype(BF16))
            delta = jnp.sum((gt * at_t[h].astype(F32))[h * 64:h * 64 + 64], axis=0, keepdims=True)
            ds.append((p[h] * (dp[h] - delta)).astype(BF16))
        dq_t = [nn(kt, ds[h]).astype(BF16) for h in range(2)]
        att[:, pl.ds(at, 128)] = jnp.where(top, *at_t).T
        dproj[:, pl.ds(at, 128)] = jnp.where(top, *dq_t).T
        dproj[:, pl.ds(pl.multiple_of(at + D, 128), 128)] = jnp.where(lane, nn(ds[0], q2), nn(ds[1], q2)).astype(BF16)
        dproj[:, pl.ds(pl.multiple_of(at + 2 * D, 128), 128)] = jnp.where(lane, nn(pb[0], g2), nn(pb[1], g2)).astype(BF16)
        return 0
    lax.fori_loop(0, 8, body, 0, unroll=4)


def columns(w, quad, lanes, width):
    four = w[:, :, pl.ds(4 * quad, 4), :, lanes]
    return jnp.concatenate([four[:, :, 2 * k:2 * k + 2].reshape(D, width) for k in range(2)], axis=1)


def project_stage(quad, nrm, w, proj):
    proj[:, pl.ds(pl.multiple_of(quad * 768, 256), 768)] = nn(nrm[...], columns(w, quad, slice(0, 384), 384)).astype(BF16)


def grad_attended_stage(quad, start, g, w, gaf):
    more = nt(g[:, pl.ds(pl.multiple_of(quad * 256, 256), 256)], columns(w, quad, slice(384, 512), 128))
    gaf[...] = more if start else gaf[...] + more


def result_stage(cnt, t_ref, att, w, out):
    live = (lax.broadcasted_iota(jnp.int32, (ROWS, 1), 0) // 8 < cnt).astype(F32)

    def body(n, _):
        c = pl.ds(pl.multiple_of(n * 256, 256), 256)
        x = t_ref[:, 0, :, c].astype(F32).reshape(ROWS, 256)
        out[:, 0, :, c] = (x + live * nn(att[...], columns(w, n, slice(384, 512), 128))).astype(BF16).reshape(32, 8, 256)
        return 0
    lax.fori_loop(0, 4, body, 0)


def grad_stage(t_ref, dproj, w, xhat, rstd, gain_ref, gn, out):
    def body(n, _):
        four = w[pl.ds(n * 4, 4), :, :, :, 0:384]
        rows = jnp.concatenate([four[:, :, 2 * m:2 * m + 2].reshape(256, 384) for m in range(8)], axis=1)
        gn[:, pl.ds(pl.multiple_of(n * 256, 256), 256)] = nt(dproj[...], rows)
        return 0
    lax.fori_loop(0, 4, body, 0)

    def last(i, _):
        s = pl.ds(pl.multiple_of(i * 32, 32), 32)
        h = xhat[s, :]
        dy = gn[s, :] * gain_ref[...]
        a = jnp.mean(dy, axis=-1, keepdims=True)
        b = jnp.mean(dy * h, axis=-1, keepdims=True)
        dx = rstd[s, 0:1] * (dy - a - h * b)
        f = pl.ds(i * 4, 4)
        x = t_ref[f, 1].astype(F32).reshape(32, D)
        out[f, 1] = (x + dx).astype(BF16).reshape(4, 8, D)
        return 0
    lax.fori_loop(0, 8, last, 0)


SCRATCH = [
    pltpu.VMEM((ROWS, D), BF16),
    pltpu.VMEM((ROWS, D), F32),
    pltpu.VMEM((ROWS, 128), F32),
    pltpu.VMEM((ROWS, D), BF16),
    pltpu.VMEM((ROWS, ROWS), F32),
    pltpu.VMEM((ROWS, 3 * D), BF16),
    pltpu.VMEM((ROWS, D), BF16),
    pltpu.VMEM((ROWS, D), BF16),
    pltpu.VMEM((ROWS, 3 * D), BF16),
    pltpu.VMEM((ROWS, D), F32),
]


MESH = pl.DeviceIdType.MESH
WORKERS = 25
VMEM_MB = 56
WAVES = (0, 3, 1, 2)


def worker_of(f):
    chip, core = f // 2, f % 2
    return (1 - core) * chip + core * (16 + (13 * chip) % 16)


def spot_of(j):
    return (2 * j) if j < 16 else 2 * ((5 * (j - 16)) % 16) + 1


def block_kernel(cnt_ref, gain_ref, tok_hbm, cot_hbm, win_hbm, wout_hbm, res_ref, grad_ref,
                 tok_ref, cot_ref, win_ref, wout_ref, xs, t_ref, y_ref, z_ref, wz, pz, w, work,
                 in_sem, tx_send, tx_recv, own_sem, z_send, z_recv, s_send, s_recv,
                 ry_send, ry_recv):
    c, f = lax.axis_index("clip"), lax.axis_index("frame")
    chip, core, par = f // 2, f % 2, c % 2
    quad = c // 4
    twin = f + 1 - 2 * core
    loads = [pltpu.make_async_copy(src, dst, in_sem.at[k]) for k, (src, dst) in enumerate(
        ((win_hbm, win_ref), (wout_hbm, wout_ref), (tok_hbm.at[0, 0], tok_ref), (cot_hbm.at[0, 0], cot_ref)))]
    for load in loads:
        load.start()
    barrier = pltpu.get_barrier_semaphore()

    def hail(i, _):
        pl.semaphore_signal(barrier, inc=1, device_id=(c, (f + i) % 32), device_id_type=MESH)
        return 0
    zs = [(c + 4) % 16, (c + 12) % 16, (c + 8) % 16] + [4 * quad + (c + d) % 4 for d in (1, 2, 3)]
    for z in zs:
        pl.semaphore_signal(barrier, inc=1, device_id=(z, f), device_id_type=MESH)
    lax.fori_loop(1, 32, hail, 0)
    for load in loads:
        load.wait()
    wz[:, 0:192] = win_ref[...]
    wz[:, 192:256] = wout_ref[...]
    for src, at in ((tok_ref, 0), (cot_ref, 1)):
        xs[0:24, at] = src[0:192].reshape(24, 8, D)
        xs[24, at, 0:4] = src[192:196]
        xs[24, at, 4:8] = jnp.zeros((4, D), BF16)
    pl.semaphore_wait(barrier, 37)

    def remote(src, dst, send_sem, recv_sem, to):
        return pltpu.make_async_remote_copy(
            src_ref=src, dst_ref=dst, send_sem=send_sem, recv_sem=recv_sem, device_id=to, device_id_type=MESH)

    swap = remote(wz.at[pl.ds(16 * (1 - par), 16)], pz, z_send.at[6], z_recv.at[6], (c + 1 - 2 * par, f))
    swap.start()

    def tx(i):
        peer = (f + i) % 32
        j = worker_of(peer)
        return j, remote(xs.at[jnp.minimum(j, WORKERS - 1)], t_ref.at[f], tx_send.at[i], tx_recv.at[i], (c, peer))

    mine = worker_of(f)

    def tx_start(i, _):
        j, copy = tx(i)

        @pl.when(j < WORKERS)
        def _():
            copy.start()
        return 0

    own = pltpu.make_async_copy(xs.at[jnp.minimum(mine, WORKERS - 1)], t_ref.at[f], own_sem)

    lax.fori_loop(1, 32, tx_start, 0)
    own.start()

    swap.wait_recv()
    low = lax.broadcasted_iota(jnp.int32, (16, 128), 1) < 64
    here = wz[pl.ds(16 * par, 16), :].astype(F32)
    there = pz[...].astype(F32)
    first, second = jnp.where(par == 0, here, there), jnp.where(par == 0, there, here)
    a0, a1, b0, b1 = first[:, :128], first[:, 128:], second[:, :128], second[:, 128:]
    turned = pltpu.roll(b0, 64, 1)
    parts = (a0, jnp.where(low, a1, turned), jnp.where(low, turned, pltpu.roll(b1, 64, 1)), jnp.where(low, pltpu.roll(a1, 64, 1), b1))
    for k in range(4):
        w[chip, core, c, :, 128 * k:128 * k + 128] = parts[k].astype(BF16)

    def far(k):
        ref = w.at[chip, core, c]
        return remote(ref, ref, z_send.at[k], z_recv.at[k], (zs[k], f))

    def near(wave, k):
        ref = w.at[chip, core, 4 * ((quad + WAVES[wave]) % 4) + c % 4]
        n = 7 + 3 * wave + k
        return remote(ref, ref, z_send.at[n], z_recv.at[n], (zs[3 + k], f))

    for k in (2, 0, 1):
        far(k).start()
    for k in range(3):
        near(0, k).start()

    s1, s2 = 4 - 3 * core, 1 + 3 * core
    x, y = chip // 4, chip % 4
    a = x * (1 - core) + y * core
    b = y * (1 - core) + x * core

    def spot(da, db):
        return ((a + da) % 4) * s1 + ((b + db) % 4) * s2

    def theirs(da, db):
        return ((b + da) % 4) * s2 + ((a + db) % 4) * s1

    sent = []
    count = [0] * 4

    def block(wave, at, half, of_core):
        first = 4 * ((quad + WAVES[wave]) % 4)
        return w.at[at, of_core, pl.ds(first, 4) if half is None else pl.ds(first + 2 * half, 2)]

    def send(wave, at, to, sem, half=None):
        ref = block(wave, at, half, core)
        copy = remote(ref, ref, s_send.at[36 * wave + count[wave]], s_recv.at[36 * wave + sem], (c, to))
        copy.start()
        sent.append(copy)
        count[wave] += 1

    def take(wave, at, sem, half=None, of_core=core):
        ref = block(wave, at, half, of_core)
        remote(ref, ref, s_send.at[36 * wave], s_recv.at[36 * wave + sem], (c, twin)).wait_recv()

    an, ap, bn, bp = spot(-1, 0), spot(1, 0), spot(0, -1), spot(0, 1)
    to_an, to_ap, to_bn, to_bp = (2 * v + core for v in (an, ap, bn, bp))
    row = (0, -1, 1, 2)

    def along_b(v, n):
        send(v, spot(row[n], 0), to_bp, 4 + 4 * n)
        send(v, spot(row[n], 0), to_bn, 4 + 4 * n + 1)

    def own_out(v):
        for k in range(3):
            near(v, k).wait_recv()
        send(v, chip, to_ap, 0)
        send(v, chip, to_an, 1)
        along_b(v, 0)
        send(v, chip, twin, 20)

    def along_a(v):
        take(v, an, 0)
        send(v, an, to_ap, 2, 0)
        along_b(v, 1)
        send(v, an, twin, 21)
        take(v, ap, 1)
        send(v, ap, to_an, 3, 1)
        along_b(v, 2)
        send(v, ap, twin, 22)

    def across_a(v):
        take(v, spot(2, 0), 2, 0)
        take(v, spot(2, 0), 3, 1)
        along_b(v, 3)
        send(v, spot(2, 0), twin, 23)

    def from_b(v, n):
        take(v, spot(row[n], -1), 4 + 4 * n)
        send(v, spot(row[n], -1), to_bp, 4 + 4 * n + 2, 0)
        send(v, spot(row[n], -1), twin, 24 + 3 * n)
        take(v, spot(row[n], 1), 4 + 4 * n + 1)
        send(v, spot(row[n], 1), to_bn, 4 + 4 * n + 3, 1)
        send(v, spot(row[n], 1), twin, 25 + 3 * n)

    def across_b(v, n):
        take(v, spot(row[n], 2), 4 + 4 * n + 2, 0)
        take(v, spot(row[n], 2), 4 + 4 * n + 3, 1)
        send(v, spot(row[n], 2), twin, 26 + 3 * n)

    def pass_on(v, k):
        far(k).wait_recv()
        for i in range(3):
            near(v, i).start()

    cnt = cnt_ref[0]
    nrm, xhat, rstd, g, bias, proj, ga, att, dproj, gn = work

    def tokens_in():
        @pl.when(mine < WORKERS)
        def _():
            def tx_wait(i, _):
                remote(xs.at[0], t_ref.at[(f - i + 32) % 32], tx_send.at[i], tx_recv.at[i], (c, twin)).wait_recv()
                return 0
            lax.fori_loop(1, 32, tx_wait, 0)
        own.wait()

        @pl.when(mine < WORKERS)
        def _():
            norm_stage(t_ref, nrm, xhat, rstd, gain_ref)
            mask_stage(cnt, t_ref, g, bias)

    def finish(v):
        for n in range(4):
            take(v, theirs(row[n], 0), 20 + n, of_core=1 - core)
        for n in range(4):
            for k, db in enumerate((-1, 1, 2)):
                take(v, theirs(row[n], db), 24 + 3 * n + k, of_core=1 - core)

        @pl.when(mine < WORKERS)
        def _():
            project_stage((quad + WAVES[v]) % 4, nrm, w, proj)
            grad_attended_stage((quad + WAVES[v]) % 4, v == 0, g, w, gn)

    pass_on(1, 0)
    pass_on(2, 1)
    own_out(0)
    pass_on(3, 2)
    along_a(0)
    own_out(1)
    own_out(2)
    from_b(0, 0)
    across_a(0)
    own_out(3)
    along_a(1)
    along_a(2)
    from_b(0, 1)
    from_b(0, 2)
    along_a(3)
    from_b(1, 0)
    from_b(2, 0)
    across_a(1)
    across_a(2)
    from_b(0, 3)
    from_b(3, 0)
    across_a(3)
    across_b(0, 0)
    from_b(1, 1)
    from_b(2, 1)
    from_b(1, 2)
    from_b(2, 2)
    across_b(0, 1)
    across_b(0, 2)
    from_b(3, 1)
    from_b(3, 2)
    from_b(1, 3)
    from_b(2, 3)
    from_b(3, 3)
    across_b(0, 3)
    for v in (1, 2):
        for n in range(4):
            across_b(v, n)
    tokens_in()
    finish(0)
    for n in range(4):
        across_b(3, n)
    for v in (1, 2, 3):
        finish(v)

    slot = jnp.minimum(mine, WORKERS - 1)

    def back(i, part):
        peer = (f + i) % 32
        return remote(y_ref.at[peer, part], z_ref.at[part, slot], ry_send.at[part, i], ry_recv.at[part, i], (c, peer))

    def give(part):
        def start(i, _):
            back(i, part).start()
            return 0
        pltpu.make_async_copy(y_ref.at[f, part], z_ref.at[part, slot], ry_send.at[part, 0]).start()
        lax.fori_loop(1, 32, start, 0)

    @pl.when(mine < WORKERS)
    def _():
        ga[...] = gn[...].astype(BF16)
        attention_stage(proj, ga, att, dproj, bias)
        result_stage(cnt, t_ref, att, w, y_ref)
        give(0)
        grad_stage(t_ref, dproj, w, xhat, rstd, gain_ref, gn, y_ref)
        give(1)

    for part, ref in ((0, res_ref), (1, grad_ref)):
        def wait(i, _):
            j = worker_of((f - i + 32) % 32)

            @pl.when(j < WORKERS)
            def _():
                remote(y_ref.at[0, part], z_ref.at[part, jnp.minimum(j, WORKERS - 1)],
                       ry_send.at[part, i], ry_recv.at[part, i], (c, twin)).wait_recv()
            return 0
        lax.fori_loop(1, 32, wait, 0)

        @pl.when(mine < WORKERS)
        def _():
            pltpu.make_async_copy(y_ref.at[f, part], z_ref.at[part, slot], ry_send.at[part, 0]).wait()
        ref[0, 0, 0:192] = z_ref[part, 0:24].reshape(192, D)
        ref[0, 0, 192:196] = z_ref[part, 24, 0:4]

    @pl.when(mine < WORKERS)
    def _():
        def back_done(i, _):
            back(i, 0).wait_send()
            back(i, 1).wait_send()
            return 0
        lax.fori_loop(1, 32, back_done, 0)

    def tx_done(i, _):
        j, copy = tx(i)

        @pl.when(j < WORKERS)
        def _():
            copy.wait_send()
        return 0
    lax.fori_loop(1, 32, tx_done, 0)

    swap.wait_send()
    for k in range(3):
        far(k).wait_send()
        for v in range(4):
            near(v, k).wait_send()
    for copy in sent:
        copy.wait_send()


def per_device(tokens, counts, norm_gain, input_weights, output_weights, cotangent):
    dma = pltpu.SemaphoreType.DMA
    vm = pl.BlockSpec(memory_space=pltpu.VMEM)
    hbm = pl.BlockSpec(memory_space=pl.ANY)
    return tuple(pl.pallas_call(
        block_kernel,
        out_shape=(jax.ShapeDtypeStruct((1, 1, 196, D), BF16),) * 2,
        in_specs=[pl.BlockSpec(memory_space=pltpu.SMEM), vm, hbm, hbm, hbm, hbm], out_specs=(vm, vm),
        scratch_shapes=[
            pltpu.VMEM((196, D), BF16), pltpu.VMEM((196, D), BF16), pltpu.VMEM((32, 192), BF16), pltpu.VMEM((32, 64), BF16),
            pltpu.VMEM((WORKERS, 2, 8, D), BF16), pltpu.VMEM((32, 2, 8, D), BF16), pltpu.VMEM((32, 2, 8, D), BF16),
            pltpu.VMEM((2, WORKERS, 8, D), BF16), pltpu.VMEM((32, 256), BF16), pltpu.VMEM((16, 256), BF16),
            pltpu.VMEM((16, 2, 16, 16, 512), BF16), SCRATCH,
            dma((4,)), dma((32,)), dma((32,)), dma, dma((19,)), dma((19,)), dma((144,)), dma((144,)),
            dma((2, 32)), dma((2, 32))],
        compiler_params=pltpu.CompilerParams(collective_id=0, has_side_effects=True, vmem_limit_bytes=VMEM_MB << 20),
        name="temporal_block",
    )(counts, norm_gain.reshape(1, D), tokens, cotangent, input_weights, output_weights))


def solution(mesh):
    rows = P("clip", "frame", None, None)
    return jax.shard_map(
        per_device, mesh=mesh,
        in_specs=(rows, P("clip"), P(), P("frame", "clip"), P("frame", "clip"), rows),
        out_specs=(rows, rows), check_vma=False)
```

time: 100 us -> 90.6 us (0.906); the launches traced: 98.8 us -> 90.4 us
  Pallas kernels: 94.9 us -> 86.5 us
    pallas_call x1, Pallas kernels: 94.9 us -> 86.5 us  [per_device(): pl.pallas_call(block_kernel, out_shape=(jax.ShapeDtypeStruct((1, 1, 196,...]
where the time goes in v3:
time: 90.6 us; the launch traced here: 90.4 us
  Pallas kernels  86.5 us (95%)
  local copies, waits for them, and re-layouts  2.59 us (3%)
  between operations  1.29 us (1%)
    pallas_call x1, Pallas kernels, per_device(): pl.pallas_call(block_kernel, out_shape=(jax.ShapeDtypeStruct((1, 1, 196,...  86.5 us
    unnamed x4, local copies, waits for them, and re-layouts  2.59 us

profile of v3, /device:TPU:25, one launch (start us, length us, event | category | flops | bytes accessed | tf_op | source)
XLA Modules:
  0.0 90.4 jit_solution(6266123487431093706)
XLA Ops:
  1.3 86.5 %temporal_block.1 = (bf16[1,1,196,1024]{3,2,1,0:T(8,128)(2,1)}, bf16[1,1,196,1024]{3,2,1,0:T(8,128)(2,1)}) custom-call(s32[1]{0:T(128)S(6)} %copy.10.cnt_ref, f32[1,1024]{1,0:T(1,128)} %bitcast.1, bf16[1,1,196,1024]{3,2,1,0:T(8,128)(2,1)} %tok_hbm.1, bf16[1,1,196,1024]{3,2,1,0:T(8,128)(2,1)} %cot_hbm.1, bf16[32,192]{1,0:T(8,128)(2,1)} %win_hbm.1, ...), custom_call_target="tpu_custom_call" | custom-call | tf_op jit(solution)/shard_map/temporal_block/pallas_call | solution.py:464
  87.8 0.0 copy-start
  87.8 1.8 %copy.11 = bf16[1,1,196,1024]{3,2,1,0:T(8,128)(2,1)} copy(bf16[1,1,196,1024]{3,2,1,0:T(8,128)(2,1)} %get-tuple-element.4) | data formatting | bytes 802816
  89.6 0.0 copy-done
  89.6 0.8 copy.12
Async XLA Ops:
  87.8 1.8 %copy-start = (bf16[1,1,196,1024]{3,2,1,0:T(8,128)(2,1)S(1)}, bf16[1,1,196,1024]{3,2,1,0:T(8,128)(2,1)}, u32[]{:S(2)}) copy-start(bf16[1,1,196,1024]{3,2,1,0:T(8,128)(2,1)} %get-tuple-element.5) | copy-start | bytes 1204228

commit v4 on v3

--- a/solution.py
+++ b/solution.py
@@ -77,7 +77,7 @@
         dproj[:, pl.ds(pl.multiple_of(at + D, 128), 128)] = jnp.where(lane, nn(ds[0], q2), nn(ds[1], q2)).astype(BF16)
         dproj[:, pl.ds(pl.multiple_of(at + 2 * D, 128), 128)] = jnp.where(lane, nn(pb[0], g2), nn(pb[1], g2)).astype(BF16)
         return 0
-    lax.fori_loop(0, 8, body, 0, unroll=4)
+    lax.fori_loop(0, 8, body, 0, unroll=8)
 
 
 def columns(w, quad, lanes, width):
@@ -105,7 +105,7 @@
     lax.fori_loop(0, 4, body, 0)
 
 
-def grad_stage(t_ref, dproj, w, xhat, rstd, gain_ref, gn, out):
+def grad_stage(t_ref, dproj, w, xhat, rstd, gain_ref, gn, out, first, made):
     def body(n, _):
         four = w[pl.ds(n * 4, 4), :, :, :, 0:384]
         rows = jnp.concatenate([four[:, :, 2 * m:2 * m + 2].reshape(256, 384) for m in range(8)], axis=1)
@@ -113,7 +113,8 @@
         return 0
     lax.fori_loop(0, 4, body, 0)
 
-    def last(i, _):
+    def last(k, _):
+        i = (first + k) % 8
         s = pl.ds(pl.multiple_of(i * 32, 32), 32)
         h = xhat[s, :]
         dy = gn[s, :] * gain_ref[...]
@@ -123,6 +124,8 @@
         f = pl.ds(i * 4, 4)
         x = t_ref[f, 1].astype(F32).reshape(32, D)
         out[f, 1] = (x + dx).astype(BF16).reshape(4, 8, D)
+        for r in range(4):
+            made(i * 4 + r)
         return 0
     lax.fori_loop(0, 8, last, 0)
 
@@ -143,7 +146,7 @@
 
 MESH = pl.DeviceIdType.MESH
 WORKERS = 25
-VMEM_MB = 56
+VMEM_MB = 53
 WAVES = (0, 3, 1, 2)
 
 
@@ -156,16 +159,16 @@
     return (2 * j) if j < 16 else 2 * ((5 * (j - 16)) % 16) + 1
 
 
-def block_kernel(cnt_ref, gain_ref, tok_hbm, cot_hbm, win_hbm, wout_hbm, res_ref, grad_ref,
-                 tok_ref, cot_ref, win_ref, wout_ref, xs, t_ref, y_ref, z_ref, wz, pz, w, work,
+def block_kernel(cnt_hbm, gain_ref, tok_hbm, cot_hbm, win_hbm, wout_hbm, res_ref, grad_ref,
+                 cnt_ref, tok_ref, cot_ref, win_ref, wout_ref, xs, t_ref, y_ref, z_ref, wz, w, work,
                  in_sem, tx_send, tx_recv, own_sem, z_send, z_recv, s_send, s_recv,
                  ry_send, ry_recv):
     c, f = lax.axis_index("clip"), lax.axis_index("frame")
-    chip, core, par = f // 2, f % 2, c % 2
+    chip, core = f // 2, f % 2
     quad = c // 4
     twin = f + 1 - 2 * core
     loads = [pltpu.make_async_copy(src, dst, in_sem.at[k]) for k, (src, dst) in enumerate(
-        ((win_hbm, win_ref), (wout_hbm, wout_ref), (tok_hbm.at[0, 0], tok_ref), (cot_hbm.at[0, 0], cot_ref)))]
+        ((win_hbm, win_ref), (wout_hbm, wout_ref), (tok_hbm.at[0, 0], tok_ref), (cot_hbm.at[0, 0], cot_ref), (cnt_hbm, cnt_ref)))]
     for load in loads:
         load.start()
     barrier = pltpu.get_barrier_semaphore()
@@ -179,8 +182,8 @@
     lax.fori_loop(1, 32, hail, 0)
     for load in loads:
         load.wait()
-    wz[:, 0:192] = win_ref[...]
-    wz[:, 192:256] = wout_ref[...]
+    wz[c, :, 0:192] = win_ref[...]
+    wz[c, :, 192:256] = wout_ref[...]
     for src, at in ((tok_ref, 0), (cot_ref, 1)):
         xs[0:24, at] = src[0:192].reshape(24, 8, D)
         xs[24, at, 0:4] = src[192:196]
@@ -191,8 +194,19 @@
         return pltpu.make_async_remote_copy(
             src_ref=src, dst_ref=dst, send_sem=send_sem, recv_sem=recv_sem, device_id=to, device_id_type=MESH)
 
-    swap = remote(wz.at[pl.ds(16 * (1 - par), 16)], pz, z_send.at[6], z_recv.at[6], (c + 1 - 2 * par, f))
-    swap.start()
+    def far(k):
+        ref = wz.at[c]
+        return remote(ref, ref, z_send.at[k], z_recv.at[k], (zs[k], f))
+
+    def near(wave, k):
+        ref = wz.at[4 * ((quad + WAVES[wave]) % 4) + c % 4]
+        n = 3 + 3 * wave + k
+        return remote(ref, ref, z_send.at[n], z_recv.at[n], (zs[3 + k], f))
+
+    for k in (2, 0, 1):
+        far(k).start()
+    for k in range(3):
+        near(0, k).start()
 
     def tx(i):
         peer = (f + i) % 32
@@ -214,30 +228,18 @@
     lax.fori_loop(1, 32, tx_start, 0)
     own.start()
 
-    swap.wait_recv()
-    low = lax.broadcasted_iota(jnp.int32, (16, 128), 1) < 64
-    here = wz[pl.ds(16 * par, 16), :].astype(F32)
-    there = pz[...].astype(F32)
-    first, second = jnp.where(par == 0, here, there), jnp.where(par == 0, there, here)
-    a0, a1, b0, b1 = first[:, :128], first[:, 128:], second[:, :128], second[:, 128:]
-    turned = pltpu.roll(b0, 64, 1)
-    parts = (a0, jnp.where(low, a1, turned), jnp.where(low, turned, pltpu.roll(b1, 64, 1)), jnp.where(low, pltpu.roll(a1, 64, 1), b1))
-    for k in range(4):
-        w[chip, core, c, :, 128 * k:128 * k + 128] = parts[k].astype(BF16)
-
-    def far(k):
-        ref = w.at[chip, core, c]
-        return remote(ref, ref, z_send.at[k], z_recv.at[k], (zs[k], f))
-
-    def near(wave, k):
-        ref = w.at[chip, core, 4 * ((quad + WAVES[wave]) % 4) + c % 4]
-        n = 7 + 3 * wave + k
-        return remote(ref, ref, z_send.at[n], z_recv.at[n], (zs[3 + k], f))
-
-    for k in (2, 0, 1):
-        far(k).start()
-    for k in range(3):
-        near(0, k).start()
+    def in_order(wave):
+        low = lax.broadcasted_iota(jnp.int32, (32, 128), 1) < 64
+        for k in range(2):
+            z = 4 * ((quad + WAVES[wave]) % 4) + 2 * k
+            first, second = wz[z].astype(F32), wz[z + 1].astype(F32)
+            a0, a1, b0, b1 = first[:, :128], first[:, 128:], second[:, :128], second[:, 128:]
+            turned = pltpu.roll(b0, 64, 1)
+            parts = (a0, jnp.where(low, a1, turned), jnp.where(low, turned, pltpu.roll(b1, 64, 1)),
+                     jnp.where(low, pltpu.roll(a1, 64, 1), b1))
+            for j in range(4):
+                for h in range(2):
+                    w[chip, core, z + h, :, 128 * j:128 * j + 128] = parts[j][16 * h:16 * h + 16].astype(BF16)
 
     s1, s2 = 4 - 3 * core, 1 + 3 * core
     x, y = chip // 4, chip % 4
@@ -279,6 +281,7 @@
     def own_out(v):
         for k in range(3):
             near(v, k).wait_recv()
+        in_order(v)
         send(v, chip, to_ap, 0)
         send(v, chip, to_an, 1)
         along_b(v, 0)
@@ -382,15 +385,23 @@
     from_b(2, 3)
     from_b(3, 3)
     across_b(0, 3)
-    for v in (1, 2):
-        for n in range(4):
-            across_b(v, n)
+    across_b(1, 0)
+    across_b(1, 1)
+    across_b(1, 2)
+    across_b(1, 3)
     tokens_in()
+    across_b(2, 0)
+    across_b(2, 1)
+    across_b(2, 2)
+    across_b(2, 3)
     finish(0)
-    for n in range(4):
-        across_b(3, n)
-    for v in (1, 2, 3):
-        finish(v)
+    across_b(3, 0)
+    across_b(3, 1)
+    across_b(3, 2)
+    across_b(3, 3)
+    finish(1)
+    finish(2)
+    finish(3)
 
     slot = jnp.minimum(mine, WORKERS - 1)
 
@@ -398,21 +409,32 @@
         peer = (f + i) % 32
         return remote(y_ref.at[peer, part], z_ref.at[part, slot], ry_send.at[part, i], ry_recv.at[part, i], (c, peer))
 
-    def give(part):
+    def keep(part):
+        return pltpu.make_async_copy(y_ref.at[f, part], z_ref.at[part, slot], ry_send.at[part, 0])
+
+    def give_result():
         def start(i, _):
-            back(i, part).start()
+            back(i, 0).start()
             return 0
-        pltpu.make_async_copy(y_ref.at[f, part], z_ref.at[part, slot], ry_send.at[part, 0]).start()
+        keep(0).start()
         lax.fori_loop(1, 32, start, 0)
+
+    def give_grad(frame):
+        @pl.when(frame == f)
+        def _():
+            keep(1).start()
+
+        @pl.when(frame != f)
+        def _():
+            back((frame + 32 - f) % 32, 1).start()
 
     @pl.when(mine < WORKERS)
     def _():
         ga[...] = gn[...].astype(BF16)
         attention_stage(proj, ga, att, dproj, bias)
         result_stage(cnt, t_ref, att, w, y_ref)
-        give(0)
-        grad_stage(t_ref, dproj, w, xhat, rstd, gain_ref, gn, y_ref)
-        give(1)
+        give_result()
+        grad_stage(t_ref, dproj, w, xhat, rstd, gain_ref, gn, y_ref, f // 4, give_grad)
 
     for part, ref in ((0, res_ref), (1, grad_ref)):
         def wait(i, _):
@@ -427,7 +449,7 @@
 
         @pl.when(mine < WORKERS)
         def _():
-            pltpu.make_async_copy(y_ref.at[f, part], z_ref.at[part, slot], ry_send.at[part, 0]).wait()
+            keep(part).wait()
         ref[0, 0, 0:192] = z_ref[part, 0:24].reshape(192, D)
         ref[0, 0, 192:196] = z_ref[part, 24, 0:4]
 
@@ -448,7 +470,6 @@
         return 0
     lax.fori_loop(1, 32, tx_done, 0)
 
-    swap.wait_send()
     for k in range(3):
         far(k).wait_send()
         for v in range(4):
@@ -464,13 +485,13 @@
     return tuple(pl.pallas_call(
         block_kernel,
         out_shape=(jax.ShapeDtypeStruct((1, 1, 196, D), BF16),) * 2,
-        in_specs=[pl.BlockSpec(memory_space=pltpu.SMEM), vm, hbm, hbm, hbm, hbm], out_specs=(vm, vm),
+        in_specs=[hbm, vm, hbm, hbm, hbm, hbm], out_specs=(vm, vm),
         scratch_shapes=[
-            pltpu.VMEM((196, D), BF16), pltpu.VMEM((196, D), BF16), pltpu.VMEM((32, 192), BF16), pltpu.VMEM((32, 64), BF16),
+            pltpu.SMEM((1,), jnp.int32), pltpu.VMEM((196, D), BF16), pltpu.VMEM((196, D), BF16), pltpu.VMEM((32, 192), BF16), pltpu.VMEM((32, 64), BF16),
             pltpu.VMEM((WORKERS, 2, 8, D), BF16), pltpu.VMEM((32, 2, 8, D), BF16), pltpu.VMEM((32, 2, 8, D), BF16),
-            pltpu.VMEM((2, WORKERS, 8, D), BF16), pltpu.VMEM((32, 256), BF16), pltpu.VMEM((16, 256), BF16),
+            pltpu.VMEM((2, WORKERS, 8, D), BF16), pltpu.VMEM((16, 32, 256), BF16),
             pltpu.VMEM((16, 2, 16, 16, 512), BF16), SCRATCH,
-            dma((4,)), dma((32,)), dma((32,)), dma, dma((19,)), dma((19,)), dma((144,)), dma((144,)),
+            dma((5,)), dma((32,)), dma((32,)), dma, dma((15,)), dma((15,)), dma((144,)), dma((144,)),
             dma((2, 32)), dma((2, 32))],
         compiler_params=pltpu.CompilerParams(collective_id=0, has_side_effects=True, vmem_limit_bytes=VMEM_MB << 20),
         name="temporal_block",

time: 90.6 us -> 89.6 us (0.989)
  Pallas kernels: 86.5 us -> 84.4 us
  local copies, waits for them, and re-layouts: 2.59 us -> 3.6 us
    pallas_call x1, Pallas kernels: 86.5 us -> 84.4 us  [per_device(): pl.pallas_call(block_kernel, out_shape=(jax.ShapeDtypeStruct((1, 1, 196,...]
    unnamed x4 -> x8, local copies, waits for them, and re-layouts: 2.59 us -> 3.6 us
where the time goes in v4:
time: 89.6 us; the launch traced here: 89.3 us
  Pallas kernels  84.4 us (94%)
  local copies, waits for them, and re-layouts  3.6 us (4%)
  between operations  1.3 us (1%)
    pallas_call x1, Pallas kernels, per_device(): pl.pallas_call(block_kernel, out_shape=(jax.ShapeDtypeStruct((1, 1, 196,...  84.4 us
    unnamed x8, local copies, waits for them, and re-layouts  3.6 us

profile of v4, /device:TPU:25, one launch (start us, length us, event | category | flops | bytes accessed | tf_op | source)
XLA Modules:
  0.0 89.3 jit_solution(580999575968585437)
XLA Ops:
  1.3 0.0 copy-start
  1.3 0.7 copy-done
  2.0 0.0 copy-start.1
  2.0 0.7 copy-done.1
  2.7 0.0 copy-start.2
  2.7 0.7 copy-done.2
  3.4 84.4 %temporal_block.1 = (bf16[1,1,196,1024]{3,2,1,0:T(8,128)(2,1)S(1)}, bf16[1,1,196,1024]{3,2,1,0:T(8,128)(2,1)S(1)}) custom-call(s32[1]{0:T(128)S(6)} %copy.10.cnt_hbm, f32[1,1024]{1,0:T(1,128)S(1)} %bitcast.1, bf16[1,1,196,1024]{3,2,1,0:T(8,128)(2,1)} %tok_hbm.1, bf16[1,1,196,1024]{3,2,1,0:T(8,128)(2,1)} %cot_hbm.1, bf16[32,192]{1,0:T(8,128)(2,1)S(1)} %copy-done, ...), custom_call_target="tpu_custom_call" | custom-call | tf_op jit(solution)/shard_map/temporal_block/pallas_call | solution.py:485
  87.8 0.8 copy.11
  88.6 0.8 copy.12
Async XLA Ops:
  1.3 0.7 copy-start
  2.0 0.7 copy-start.1
  2.7 0.7 copy-start.2
